TPU v7x, 32 devices: a whole 2x2x4 slice. The times are simulated.
32 devices in a mesh: gx: 4 (over y, core), gy: 8 (over z, x).
Axes of the slice: x: 2, y: 2, z: 4, core: 2. Of those that a mesh axis runs over, the one named last changes fastest.
Arguments:
- rhs_blocks: bfloat16 [32, 64, 64, 128], P('gx', 'gy'), may hold values from -6 to 6
- diag_factor: bfloat16 [32, 64, 128, 128], P('gx', 'gy'), as said below
- cond_factor: bfloat16 [32, 64, 6, 128, 128], P('gx', 'gy'), may hold values from -0.21875 to 0.21875
- cond: int32 [32, 64, 6], P('gx', 'gy'), may hold values from 0 to 24, as said below
Outputs:
- precision_times: float32 [32, 64, 64, 128], P('gx', 'gy')
Inputs may be any that keep to these rules, and one draw needn't show every extreme that they name: `cond`: each block's 6 codes are distinct, never 12, and name blocks inside the grid of 32 x 64 blocks. `diag_factor`: each matrix is upper triangular with a positive diagonal.
All inputs are finite; a program needn't handle non-finite values.
Results may differ from a plain program's by a relative error of at most 0.0023.
Values may be sent and summed in bfloat16 or wider, within the bound.
A program may use at most 192 MiB of HBM per device.

v0:
```python
import jax
import jax.numpy as jnp
from jax import lax
from jax.sharding import PartitionSpec as P


def extended(cells, sides, width):
    for axis, dim in sides:
        count = lax.axis_size(axis)
        ends = count - 1
        head = lax.slice_in_dim(cells, 0, width, axis=dim)
        tail = lax.slice_in_dim(cells, cells.shape[dim] - width, cells.shape[dim], axis=dim)
        cells = jnp.concatenate(
            [
                lax.ppermute(tail, axis, [(i, (i + 1) % count) for i in range(ends)]),
                cells,
                lax.ppermute(head, axis, [((i + 1) % count, i) for i in range(ends)]),
            ],
            axis=dim,
        )
    return cells


def from_behind(value, axis, steps):
    count = lax.axis_size(axis)
    first, last = (max(0, -steps), min(count, count - steps))
    return lax.ppermute(value, axis, [(source, source + steps) for source in range(first, last)])


def shards(rhs_blocks, diag_factor, cond_factor, cond):
    tile_rows, tile_cols, count_rhs, point_count = rhs_blocks.shape
    padded = extended(rhs_blocks, (("gx", 0), ("gy", 1)), 2)
    code_list = [code for code in range(25) if code != 12]
    picked = jnp.zeros(
        (tile_rows, tile_cols, cond.shape[2], count_rhs, point_count), rhs_blocks.dtype
    )
    for code in code_list:
        off_row = code // 5
        off_col = code % 5
        window = padded[off_row : off_row + tile_rows, off_col : off_col + tile_cols]
        picked = jnp.where((cond == code)[:, :, :, None, None], window[:, :, None], picked)
    own_mixed = jnp.einsum(
        "xyrp,xypq->xyrq", rhs_blocks, diag_factor, preferred_element_type=jnp.float32
    )
    far_mixed = jnp.einsum(
        "xykrp,xykpq->xyrq", picked, cond_factor, preferred_element_type=jnp.float32
    )
    whitened = (own_mixed + far_mixed).astype(jnp.bfloat16)
    own_part = jnp.einsum(
        "xyrq,xypq->xyrp", whitened, diag_factor, preferred_element_type=jnp.float32
    )
    spread = jnp.einsum(
        "xyrq,xykpq->xykrp", whitened, cond_factor, preferred_element_type=jnp.float32
    )
    accumulated = jnp.zeros((tile_rows + 4, tile_cols + 4, count_rhs, point_count), jnp.float32)
    for code in code_list:
        off_row = code // 5
        off_col = code % 5
        matched = (cond == code)[:, :, :, None, None]
        contrib = jnp.sum(jnp.where(matched, spread, 0.0), axis=2)
        accumulated = accumulated.at[
            off_row : off_row + tile_rows, off_col : off_col + tile_cols
        ].add(contrib)
    row_source = {-1: (0, 2), 0: (2, tile_rows + 2), 1: (tile_rows + 2, tile_rows + 4)}
    row_target = {-1: (tile_rows - 2, tile_rows), 0: (0, tile_rows), 1: (0, 2)}
    col_source = {-1: (0, 2), 0: (2, tile_cols + 2), 1: (tile_cols + 2, tile_cols + 4)}
    col_target = {-1: (tile_cols - 2, tile_cols), 0: (0, tile_cols), 1: (0, 2)}
    interior = accumulated[2 : tile_rows + 2]
    for direction in (-1, 1):
        row_start, row_end = row_source[direction]
        arrived = from_behind(accumulated[row_start:row_end], "gx", direction)
        row_first, row_last = row_target[direction]
        interior = interior.at[row_first:row_last].add(arrived)
    core_part = interior[:, 2 : tile_cols + 2]
    for direction in (-1, 1):
        col_start, col_end = col_source[direction]
        arrived = from_behind(interior[:, col_start:col_end], "gy", direction)
        col_first, col_last = col_target[direction]
        core_part = core_part.at[:, col_first:col_last].add(arrived)
    return own_part + core_part


def solution(mesh):
    in_specs = (
        P("gx", "gy", None, None),
        P("gx", "gy", None, None),
        P("gx", "gy", None, None, None),
        P("gx", "gy", None),
    )
    out_specs = P("gx", "gy", None, None)
    return jax.shard_map(shards, mesh=mesh, in_specs=in_specs, out_specs=out_specs, check_vma=False)
```

profile of v0, /device:TPU:9, one launch (start us, length us, event | category | flops | bytes accessed | tf_op | source)
XLA Modules:
  0.0 205.6 jit_solution(5305881109682188794)
XLA Ops:
  1.2 2.7 %collective-permute-start.1 = (bf16[2,8,64,128]{3,2,1,0:T(8,128)(2,1)S(1)}, bf16[2,8,64,128]{3,2,1,0:T(8,128)(2,1)S(1)}, u32[]{:S(2)}, u32[]{:S(2)}) collective-permute-start(bf16[2,8,64,128]{3,2,1,0:T(8,128)(2,1)S(1)} %get-tuple-element.400), channel_id=1, source_target_pairs={{8,0},{16,8},{24,16},{9,1},{17,9},{25,17},{10,2},{18,10},{26,18},{... | collective-permute-start | bytes 786440 | tf_op jit(solution)/shard_map/ppermute | solution.py:17
  4.0 3.0 %collective-permute-start = (bf16[2,8,64,128]{3,2,1,0:T(8,128)(2,1)S(1)}, bf16[2,8,64,128]{3,2,1,0:T(8,128)(2,1)S(1)}, u32[]{:S(2)}, u32[]{:S(2)}) collective-permute-start(bf16[2,8,64,128]{3,2,1,0:T(8,128)(2,1)S(1)} %get-tuple-element.401), channel_id=1, source_target_pairs={{0,8},{8,16},{16,24},{1,9},{9,17},{17,25},{2,10},{10,18},{18,26},{... | collective-permute-start | bytes 786440 | tf_op jit(solution)/shard_map/ppermute | solution.py:15
  8.3 3.2 %fusion.134 = f32[8,8,64,128]{3,2,1,0:T(8,128)} fusion(bf16[8,8,64,128]{3,2,1,0:T(8,128)(2,1)} %param.60, bf16[8,8,128,128]{3,2,1,0:T(8,128)(2,1)S(1)} %copy-done), kind=kOutput, calls=%fused_computation.266 | convolution fusion | flops 134217728 | bytes 5242880 | tf_op jit(solution)/shard_map/xyrp,xypq->xyrq/dot_general | solution.py:42
  17.0 3.1 %collective-permute-start.3 = (bf16[12,2,64,128]{3,2,1,0:T(8,128)(2,1)}, bf16[12,2,64,128]{3,2,1,0:T(8,128)(2,1)}, u32[]{:S(2)}, u32[]{:S(2)}) collective-permute-start(bf16[12,2,64,128]{3,2,1,0:T(8,128)(2,1)} %get-tuple-element.392), channel_id=1, source_target_pairs={{0,1},{1,2},{2,3},{3,4},{4,5},{5,6},{6,7},{8,9},{9,10},{10,11},{11... | collective-permute-start | bytes 1179656 | tf_op jit(solution)/shard_map/ppermute | solution.py:15
  32.5 3.0 %collective-permute-start.2 = (bf16[12,2,64,128]{3,2,1,0:T(8,128)(2,1)}, bf16[12,2,64,128]{3,2,1,0:T(8,128)(2,1)S(1)}, u32[]{:S(2)}, u32[]{:S(2)}) collective-permute-start(bf16[12,2,64,128]{3,2,1,0:T(8,128)(2,1)} %get-tuple-element.391), channel_id=1, source_target_pairs={{1,0},{2,1},{3,2},{4,3},{5,4},{6,5},{7,6},{9,8},{10,9},{11,10},{12... | collective-permute-start | bytes 1179656 | tf_op jit(solution)/shard_map/ppermute | solution.py:17
  35.5 2.8 %fusion.127 = (bf16[8,8,64,128]{3,2,1,0:T(8,128)(2,1)S(1)}, bf16[8,8,64,128]{3,2,1,0:T(8,128)(2,1)S(1)}, bf16[8,8,64,128]{3,2,1,0:T(8,128)(2,1)S(1)}, bf16[8,8,64,128]{3,2,1,0:T(8,128)(2,1)S(1)}) fusion(bf16[10,8,64,128]{3,2,1,0:T(8,128)(2,1)S(1)} %get-tuple-element.402, bf16[10,8,64,128]{3,2,1,0:T(8,128)(2,1)} %copy-done.22), kind=kLoop, calls=%fused_computation.259 | loop fusion | bytes 8388608 | tf_op jit(solution)/shard_map/slice | solution.py:40
  38.3 3.3 %fusion.100 = (bf16[8,8,64,128]{3,2,1,0:T(8,128)(2,1)S(1)}, bf16[8,8,64,128]{3,2,1,0:T(8,128)(2,1)S(1)}, bf16[8,8,64,128]{3,2,1,0:T(8,128)(2,1)S(1)}, bf16[8,8,6...) fusion(bf16[12,8,64,128]{3,2,1,0:T(8,128)(2,1)S(1)} %copy-done., ...), kind=kLoop, calls=%fused_computation.183 | loop fusion | flops 4718592 | bytes 11403264 | tf_op jit(solution)/shard_map/concatenate | solution.py:13
  41.6 3.9 %collective-permute-done.2 = bf16[12,2,64,128]{3,2,1,0:T(8,128)(2,1)S(1)} collective-permute-done((bf16[12,2,64,128]{3,2,1,0:T(8,128)(2,1)}, bf16[12,2,64,128]{3,2,1,0:T(8,128)(2,1)S(1)}, u32[]{:S(2)}, u32[]{:S(2)}) %collective-permute-start.2) | collective-permute-done | bytes 393248 | tf_op jit(solution)/shard_map/ppermute | solution.py:17
  46.7 2.7 %fusion.109 = (bf16[8,8,64,128]{3,2,1,0:T(8,128)(2,1)S(1)}, bf16[8,8,64,128]{3,2,1,0:T(8,128)(2,1)S(1)}, bf16[8,8,64,128]{3,2,1,0:T(8,128)(2,1)S(1)}, bf16[8,8,6...) fusion(bf16[12,8,64,128]{3,2,1,0:T(8,128)(2,1)S(1)} %copy-done., ...), kind=kLoop, calls=%fused_computation.192 | loop fusion | flops 4718592 | bytes 11403264 | tf_op jit(solution)/shard_map/concatenate | solution.py:13
  49.4 22.1 %fusion.96 = bf16[8,8,64,128]{3,2,1,0:T(8,128)(2,1)S(1)} fusion(f32[8,8,64,128]{3,2,1,0:T(8,128)S(1)} %copy-done.24, bf16[8,8,6,128,128]{4,3,2,1,0:T(8,128)(2,1)} %param.62, pred[8,8,6]{2,1,0:T(8,128)(4,1)S(1)} %copy-done.34, pred[8,8,6]{2,1,0:T(8,128)(4,1)S(1)} %copy-done.35, pred[8,8,6]{2,1,0:T(8,128)(4,1)S(1)} %copy-done.30, ...), kind=kOutput, calls=%fused_computation.161 | convolution fusion | flops 881852416 | bytes 40903680 | tf_op jit(solution)/shard_map/xykrp,xykpq->xyrq/dot_general | solution.py:45
  71.6 16.8 %select_reduce_fusion.18 = (f32[8,8,64,128]{3,2,1,0:T(8,128)}, f32[8,8,64,128]{3,2,1,0:T(8,128)}, f32[8,8,64,128]{3,2,1,0:T(8,128)}, f32[8,8,64,128]{3,2,1,0:T(8...) fusion(pred[8,8,6]{2,1,0:T(8,128)(4,1)S(1)} %copy-done.33, ...), kind=kOutput, calls=%fused_computation.18 | convolution fusion | flops 839909376 | bytes 38799616 | tf_op jit(solution)/shard_map/xyrq,xykpq->xykrp/dot_general | solution.py:52
  88.3 37.4 %select_reduce_fusion = (f32[8,8,64,128]{3,2,1,0:T(8,128)}, f32[8,8,64,128]{3,2,1,0:T(8,128)}, f32[8,8,64,128]{3,2,1,0:T(8,128)}, f32[8,8,64,128]{3,2,1,0:T(8,12...) fusion(f32[8,8,64,6,128]{4,2,3,1,0:T(8,128)S(1)} %get-tuple-ele, ...), kind=kLoop, calls=%fused_computation | loop fusion | flops 103809024 | bytes 50338560 | tf_op jit(solution)/shard_map/reduce_sum | solution.py:60
  125.8 2.3 %scatter-add.94 = f32[12,12,64,128]{3,2,1,0:T(8,128)S(1)} pad(f32[8,8,64,128]{3,2,1,0:T(8,128)} %get-tuple-element.364, f32[]{:T(128)} %constant.863.clone.1), padding=0_4x0_4x0_0x0_0 | pad | bytes 6815748 | tf_op jit(solution)/shard_map/scatter-add | solution.py:63
  128.1 1.9 add_dynamic-update-slice_fusion
  130.0 2.5 %fusion.74 = f32[12,12,64,128]{3,2,1,0:T(8,128)S(1)} fusion(f32[12,12,64,128]{3,2,1,0:T(8,128)S(1)} %add_dynamic-update-slice_fusion, s32[]{:T(128)} %bitcast.6, s32[]{:T(128)} %bitcast.7, f32[8,8,64,128]{3,2,1,0:T(8,128)S(1)} %copy-done.27, pred[]{:T(512)} %get-tuple-element.432), kind=kLoop, calls=%fused_computation.119 | loop fusion | flops 1048576 | bytes 6291465 | tf_op jit(solution)/shard_map/scatter-add | solution.py:63
  132.5 2.5 %fusion.75 = f32[12,12,64,128]{3,2,1,0:T(8,128)S(1)} fusion(f32[12,12,64,128]{3,2,1,0:T(8,128)S(1)} %fusion.74, s32[]{:T(128)} %bitcast.8, s32[]{:T(128)} %bitcast.9, f32[8,8,64,128]{3,2,1,0:T(8,128)S(1)} %copy-done.26, pred[]{:T(512)} %get-tuple-element.366), kind=kLoop, calls=%fused_computation.120 | loop fusion | flops 1048576 | bytes 6291465 | tf_op jit(solution)/shard_map/scatter-add | solution.py:63
  135.0 2.6 %fusion.76 = f32[12,12,64,128]{3,2,1,0:T(8,128)S(1)} fusion(f32[12,12,64,128]{3,2,1,0:T(8,128)S(1)} %fusion.75, s32[]{:T(128)} %bitcast.10, s32[]{:T(128)} %bitcast.11, f32[8,8,64,128]{3,2,1,0:T(8,128)S(1)} %copy-done.25, pred[]{:T(512)} %get-tuple-element.365), kind=kLoop, calls=%fused_computation.121 | loop fusion | flops 1048576 | bytes 6291465 | tf_op jit(solution)/shard_map/scatter-add | solution.py:63
  167.2 2.4 %collective-permute-start.4 = (f32[2,12,64,128]{3,2,1,0:T(8,128)S(1)}, f32[2,12,64,128]{3,2,1,0:T(8,128)S(1)}, u32[]{:S(2)}, u32[]{:S(2)}) collective-permute-start(f32[2,12,64,128]{3,2,1,0:T(8,128)S(1)} %get-tuple-element.368), channel_id=1, source_target_pairs={{8,0},{16,8},{24,16},{9,1},{17,9},{25,17},{10,2},{18,10},{26,18},{... | collective-permute-start | bytes 2359304 | tf_op jit(solution)/shard_map/ppermute | solution.py:27
  169.6 3.1 %collective-permute-start.5 = (f32[2,12,64,128]{3,2,1,0:T(8,128)S(1)}, f32[2,12,64,128]{3,2,1,0:T(8,128)S(1)}, u32[]{:S(2)}, u32[]{:S(2)}) collective-permute-start(f32[2,12,64,128]{3,2,1,0:T(8,128)S(1)} %get-tuple-element.367), channel_id=1, source_target_pairs={{0,8},{8,16},{16,24},{1,9},{9,17},{17,25},{2,10},{10,18},{18,26},{... | collective-permute-start | bytes 2359304 | tf_op jit(solution)/shard_map/ppermute | solution.py:27
  173.2 7.6 %collective-permute-done.4 = f32[2,12,64,128]{3,2,1,0:T(8,128)S(1)} collective-permute-done((f32[2,12,64,128]{3,2,1,0:T(8,128)S(1)}, f32[2,12,64,128]{3,2,1,0:T(8,128)S(1)}, u32[]{:S(2)}, u32[]{:S(2)}) %collective-permute-start.4) | collective-permute-done | bytes 786464 | tf_op jit(solution)/shard_map/ppermute | solution.py:27
  182.0 4.0 %collective-permute-start.6 = (f32[8,2,64,128]{3,2,1,0:T(8,128)S(1)}, f32[8,2,64,128]{3,2,1,0:T(8,128)S(1)}, u32[]{:S(2)}, u32[]{:S(2)}) collective-permute-start(f32[8,2,64,128]{3,2,1,0:T(8,128)S(1)} %get-tuple-element.370), channel_id=1, source_target_pairs={{1,0},{2,1},{3,2},{4,3},{5,4},{6,5},{7,6},{9,8},{10,9},{11,10},{12... | collective-permute-start | bytes 1572872 | tf_op jit(solution)/shard_map/ppermute | solution.py:27
  185.9 2.0 collective-permute-start.7
  188.2 13.7 %collective-permute-done.6 = f32[8,2,64,128]{3,2,1,0:T(8,128)S(1)} collective-permute-done((f32[8,2,64,128]{3,2,1,0:T(8,128)S(1)}, f32[8,2,64,128]{3,2,1,0:T(8,128)S(1)}, u32[]{:S(2)}, u32[]{:S(2)}) %collective-permute-start.6) | collective-permute-done | bytes 524320 | tf_op jit(solution)/shard_map/ppermute | solution.py:27
  202.8 2.9 %convolution_add_fusion = f32[8,8,64,128]{3,2,1,0:T(8,128)} fusion(f32[8,8,64,128]{3,2,1,0:T(8,128)S(1)} %fusion.121, bf16[8,8,64,128]{3,2,1,0:T(8,128)(2,1)S(1)} %fusion.96, bf16[8,8,128,128]{3,2,1,0:T(8,128)(2,1)S(1)} %copy-done), kind=kOutput, calls=%fused_computation.181 | convolution fusion | flops 134742016 | bytes 7340032 | tf_op jit(solution)/shard_map/xyrq,xypq->xyrp/dot_general | solution.py:49
  (145 shorter events, 53.3 us)
Async XLA Ops:
  0.0 8.3 %copy-start = (bf16[8,8,128,128]{3,2,1,0:T(8,128)(2,1)S(1)}, bf16[8,8,128,128]{3,2,1,0:T(8,128)(2,1)}, u32[]{:S(2)}) copy-start(bf16[8,8,128,128]{3,2,1,0:T(8,128)(2,1)} %param.61) | copy-start | bytes 6291460
  0.0 11.5 %copy-start.36 = (s32[4]{0:T(128)S(1)}, s32[4]{0:T(128)}, u32[]{:S(2)}) copy-start(s32[4]{0:T(128)} %constant.865.clone.1) | copy-start | bytes 52
  0.0 12.9 %copy-start.29 = (s32[8,8,6]{1,0,2:T(8,128)S(1)}, s32[8,8,6]{1,0,2:T(8,128)}, u32[]{:S(2)}) copy-start(s32[8,8,6]{1,0,2:T(8,128)} %param.63) | copy-start | bytes 4612
  1.2 12.5 %copy-start.21 = (bf16[8,8,64,128]{3,2,1,0:T(8,128)(2,1)S(1)}, bf16[8,8,64,128]{3,2,1,0:T(8,128)(2,1)}, u32[]{:S(2)}) copy-start(bf16[8,8,64,128]{3,2,1,0:T(8,128)(2,1)} %param.60) | copy-start | bytes 3145732
  1.2 13.4 %collective-permute-start.1 = (bf16[2,8,64,128]{3,2,1,0:T(8,128)(2,1)S(1)}, bf16[2,8,64,128]{3,2,1,0:T(8,128)(2,1)S(1)}, u32[]{:S(2)}, u32[]{:S(2)}) collective-permute-start(bf16[2,8,64,128]{3,2,1,0:T(8,128)(2,1)S(1)} %get-tuple-element.400), channel_id=1, source_target_pairs={{8,0},{16,8},{24,16},{9,1},{17,9},{25,17},{10,2},{18,10},{26,18},{... | collective-permute-start | bytes 786440 | tf_op jit(solution)/shard_map/ppermute | solution.py:17
  4.0 9.6 %collective-permute-start = (bf16[2,8,64,128]{3,2,1,0:T(8,128)(2,1)S(1)}, bf16[2,8,64,128]{3,2,1,0:T(8,128)(2,1)S(1)}, u32[]{:S(2)}, u32[]{:S(2)}) collective-permute-start(bf16[2,8,64,128]{3,2,1,0:T(8,128)(2,1)S(1)} %get-tuple-element.401), channel_id=1, source_target_pairs={{0,8},{8,16},{16,24},{1,9},{9,17},{17,25},{2,10},{10,18},{18,26},{... | collective-permute-start | bytes 786440 | tf_op jit(solution)/shard_map/ppermute | solution.py:15
  14.6 2.4 %copy-start.22 = (bf16[10,8,64,128]{3,2,1,0:T(8,128)(2,1)}, bf16[10,8,64,128]{3,2,1,0:T(8,128)(2,1)S(1)}, u32[]{:S(2)}) copy-start(bf16[10,8,64,128]{3,2,1,0:T(8,128)(2,1)S(1)} %get-tuple-element.399) | copy-start | bytes 3932164
  17.0 21.2 %collective-permute-start.3 = (bf16[12,2,64,128]{3,2,1,0:T(8,128)(2,1)}, bf16[12,2,64,128]{3,2,1,0:T(8,128)(2,1)}, u32[]{:S(2)}, u32[]{:S(2)}) collective-permute-start(bf16[12,2,64,128]{3,2,1,0:T(8,128)(2,1)} %get-tuple-element.392), channel_id=1, source_target_pairs={{0,1},{1,2},{2,3},{3,4},{4,5},{5,6},{6,7},{8,9},{9,10},{10,11},{11... | collective-permute-start | bytes 1179656 | tf_op jit(solution)/shard_map/ppermute | solution.py:15
  32.5 13.1 %collective-permute-start.2 = (bf16[12,2,64,128]{3,2,1,0:T(8,128)(2,1)}, bf16[12,2,64,128]{3,2,1,0:T(8,128)(2,1)S(1)}, u32[]{:S(2)}, u32[]{:S(2)}) collective-permute-start(bf16[12,2,64,128]{3,2,1,0:T(8,128)(2,1)} %get-tuple-element.391), channel_id=1, source_target_pairs={{1,0},{2,1},{3,2},{4,3},{5,4},{6,5},{7,6},{9,8},{10,9},{11,10},{12... | collective-permute-start | bytes 1179656 | tf_op jit(solution)/shard_map/ppermute | solution.py:17
  35.5 2.8 %copy-start.2 = (bf16[12,8,64,128]{3,2,1,0:T(8,128)(2,1)S(1)}, bf16[12,8,64,128]{3,2,1,0:T(8,128)(2,1)}, u32[]{:S(2)}) copy-start(bf16[12,8,64,128]{3,2,1,0:T(8,128)(2,1)} %copy-done.1) | copy-start | bytes 4718596
  46.6 2.8 %copy-start.24 = (f32[8,8,64,128]{3,2,1,0:T(8,128)S(1)}, f32[8,8,64,128]{3,2,1,0:T(8,128)}, u32[]{:S(2)}) copy-start(f32[8,8,64,128]{3,2,1,0:T(8,128)} %fusion.134) | copy-start | bytes 6291460
  46.6 2.8 %copy-start.30 = (pred[8,8,6]{2,1,0:T(8,128)(4,1)S(1)}, pred[8,8,6]{2,1,0:T(8,128)(4,1)}, u32[]{:S(2)}) copy-start(pred[8,8,6]{2,1,0:T(8,128)(4,1)} %copy.26) | copy-start | bytes 1156
  46.6 2.8 %copy-start.31 = (pred[8,8,6]{2,1,0:T(8,128)(4,1)S(1)}, pred[8,8,6]{2,1,0:T(8,128)(4,1)}, u32[]{:S(2)}) copy-start(pred[8,8,6]{2,1,0:T(8,128)(4,1)} %copy.25) | copy-start | bytes 1156
  46.6 2.8 %copy-start.32 = (pred[8,8,6]{2,1,0:T(8,128)(4,1)S(1)}, pred[8,8,6]{2,1,0:T(8,128)(4,1)}, u32[]{:S(2)}) copy-start(pred[8,8,6]{2,1,0:T(8,128)(4,1)} %copy.24) | copy-start | bytes 1156
  46.7 2.8 %copy-start.33 = (pred[8,8,6]{2,1,0:T(8,128)(4,1)S(1)}, pred[8,8,6]{2,1,0:T(8,128)(4,1)}, u32[]{:S(2)}) copy-start(pred[8,8,6]{2,1,0:T(8,128)(4,1)} %copy.23) | copy-start | bytes 1156
  46.7 2.8 %copy-start.34 = (pred[8,8,6]{2,1,0:T(8,128)(4,1)S(1)}, pred[8,8,6]{2,1,0:T(8,128)(4,1)}, u32[]{:S(2)}) copy-start(pred[8,8,6]{2,1,0:T(8,128)(4,1)} %copy.28) | copy-start | bytes 1156
  46.7 2.8 %copy-start.35 = (pred[8,8,6]{2,1,0:T(8,128)(4,1)S(1)}, pred[8,8,6]{2,1,0:T(8,128)(4,1)}, u32[]{:S(2)}) copy-start(pred[8,8,6]{2,1,0:T(8,128)(4,1)} %copy.27) | copy-start | bytes 1156
  130.0 2.5 %copy-start.26 = (f32[8,8,64,128]{3,2,1,0:T(8,128)S(1)}, f32[8,8,64,128]{3,2,1,0:T(8,128)}, u32[]{:S(2)}) copy-start(f32[8,8,64,128]{3,2,1,0:T(8,128)} %get-tuple-element.361) | copy-start | bytes 6291460
  132.5 2.5 %copy-start.25 = (f32[8,8,64,128]{3,2,1,0:T(8,128)S(1)}, f32[8,8,64,128]{3,2,1,0:T(8,128)}, u32[]{:S(2)}) copy-start(f32[8,8,64,128]{3,2,1,0:T(8,128)} %get-tuple-element.360) | copy-start | bytes 6291460
  135.0 2.7 %copy-start.23 = (f32[8,8,64,128]{3,2,1,0:T(8,128)S(1)}, f32[8,8,64,128]{3,2,1,0:T(8,128)}, u32[]{:S(2)}) copy-start(f32[8,8,64,128]{3,2,1,0:T(8,128)} %get-tuple-element.359) | copy-start | bytes 6291460
  167.2 13.6 %collective-permute-start.4 = (f32[2,12,64,128]{3,2,1,0:T(8,128)S(1)}, f32[2,12,64,128]{3,2,1,0:T(8,128)S(1)}, u32[]{:S(2)}, u32[]{:S(2)}) collective-permute-start(f32[2,12,64,128]{3,2,1,0:T(8,128)S(1)} %get-tuple-element.368), channel_id=1, source_target_pairs={{8,0},{16,8},{24,16},{9,1},{17,9},{25,17},{10,2},{18,10},{26,18},{... | collective-permute-start | bytes 2359304 | tf_op jit(solution)/shard_map/ppermute | solution.py:27
  169.6 12.1 %collective-permute-start.5 = (f32[2,12,64,128]{3,2,1,0:T(8,128)S(1)}, f32[2,12,64,128]{3,2,1,0:T(8,128)S(1)}, u32[]{:S(2)}, u32[]{:S(2)}) collective-permute-start(f32[2,12,64,128]{3,2,1,0:T(8,128)S(1)} %get-tuple-element.367), channel_id=1, source_target_pairs={{0,8},{8,16},{16,24},{1,9},{9,17},{17,25},{2,10},{10,18},{18,26},{... | collective-permute-start | bytes 2359304 | tf_op jit(solution)/shard_map/ppermute | solution.py:27
  182.0 19.9 %collective-permute-start.6 = (f32[8,2,64,128]{3,2,1,0:T(8,128)S(1)}, f32[8,2,64,128]{3,2,1,0:T(8,128)S(1)}, u32[]{:S(2)}, u32[]{:S(2)}) collective-permute-start(f32[8,2,64,128]{3,2,1,0:T(8,128)S(1)} %get-tuple-element.370), channel_id=1, source_target_pairs={{1,0},{2,1},{3,2},{4,3},{5,4},{6,5},{7,6},{9,8},{10,9},{11,10},{12... | collective-permute-start | bytes 1572872 | tf_op jit(solution)/shard_map/ppermute | solution.py:27
  185.9 16.7 %collective-permute-start.7 = (f32[8,2,64,128]{3,2,1,0:T(8,128)S(1)}, f32[8,2,64,128]{3,2,1,0:T(8,128)S(1)}, u32[]{:S(2)}, u32[]{:S(2)}) collective-permute-start(f32[8,2,64,128]{3,2,1,0:T(8,128)S(1)} %get-tuple-element.369), channel_id=1, source_target_pairs={{0,1},{1,2},{2,3},{3,4},{4,5},{5,6},{6,7},{8,9},{9,10},{10,11},{11... | collective-permute-start | bytes 1572872 | tf_op jit(solution)/shard_map/ppermute | solution.py:27
  (21 other events, 34.2 us)
where the time goes:
time: 208 us; the launch traced here: 206 us
  other arithmetic  68.8 us (33%)
  matrix products  45 us (22%)
  local copies, waits for them, and re-layouts  41 us (20%)
  waiting for transfers between devices  26.7 us (13%)
  starting transfers between devices  23.5 us (11%)
    reduce_sum x1, other arithmetic, shards(): contrib = jnp.sum(jnp.where(matched, spread, 0.0), axis=2)  37.4 us
    ppermute x4, waiting for transfers between devices, from_behind(): lax.ppermute(value, axis, [(source, source + steps) for source in range(f...  22.7 us
    scatter-add x23, other arithmetic, shards(): accumulated = accumulated.at[off_row:off_row + tile_rows, off_col:off_col...  22.3 us
    dot_general x1, matrix products, shards(): jnp.einsum('xykrp,xykpq->xyrq', picked, cond_factor, preferred_element_ty...  22.1 us
    unnamed x76, local copies, waits for them, and re-layouts  18.7 us
    dot_general x1, matrix products, shards(): jnp.einsum('xyrq,xykpq->xykrp', whitened, cond_factor, preferred_element_...  16.8 us
    eq x24, local copies, waits for them, and re-layouts, shards(): cond == code  11.6 us
    ppermute x4, starting transfers between devices, from_behind(): lax.ppermute(value, axis, [(source, source + steps) for source in range(f...  11.6 us
  transfers between devices with their start and end apart: 8, of which 5 were waited for; matrix products, arithmetic and copies ran while one was open for 13% of the time, Pallas kernels for 0%

commit v1 on v0

v1 whole, which is shorter than its diff:
```python
import functools

import jax
import jax.numpy as jnp
from jax import lax
from jax.experimental import pallas as pl
from jax.experimental.pallas import tpu as pltpu
from jax.sharding import PartitionSpec as P

MESH = pl.DeviceIdType.MESH
REACH = 2
SPAN = 2 * REACH + 1
SIDES = [(0, -1), (0, 1), (-1, 0), (1, 0), (-1, -1), (-1, 1), (1, -1), (1, 1)]


def own_edge(step, size):
    return {-1: (0, REACH), 0: (0, size), 1: (size - REACH, REACH)}[step]


def outer_edge(step, size):
    return {-1: (0, REACH), 0: (REACH, size), 1: (REACH + size, REACH)}[step]


def at_region(ref, row_part, col_part):
    return ref.at[pl.ds(*row_part), pl.ds(*col_part)]


def neighbourhood():
    row, col = lax.axis_index("gx"), lax.axis_index("gy")
    rows, cols = lax.axis_size("gx"), lax.axis_size("gy")

    def inside(side):
        r, c = row + side[0], col + side[1]
        return (r >= 0) & (r < rows) & (c >= 0) & (c < cols)

    def device(side):
        return {"gx": row + side[0], "gy": col + side[1]}

    return inside, device


def greet(inside, device):
    barrier = pltpu.get_barrier_semaphore()
    count = jnp.int32(0)
    for side in SIDES:
        count = count + inside(side).astype(jnp.int32)

        @pl.when(inside(side))
        def _():
            pl.semaphore_signal(barrier, inc=1, device_id=device(side), device_id_type=MESH)

    pl.semaphore_wait(barrier, count)


def opposite(side):
    return (-side[0], -side[1])


def forward_kernel(rhs, diag, far, cond, white, local, padded, weights, load_sem, rhs_sem, send_sem, recv_sem):
    tile_rows, tile_cols, count_rhs, points = rhs.shape
    depth = far.shape[2]
    inside, device = neighbourhood()
    row_order = list(range(REACH, tile_rows - REACH))
    row_order += [r for r in range(tile_rows) if r not in row_order]

    def loads(r):
        return [
            pltpu.make_async_copy(far.at[r], weights.at[r, :, pl.ds(0, depth)], load_sem.at[r, 0]),
            pltpu.make_async_copy(diag.at[r], weights.at[r, :, pl.ds(depth, points)], load_sem.at[r, 1]),
        ]

    local_copy = pltpu.make_async_copy(rhs, local, rhs_sem.at[0])
    centre_copy = pltpu.make_async_copy(
        rhs, at_region(padded, (REACH, tile_rows), (REACH, tile_cols)), rhs_sem.at[1]
    )
    local_copy.start()
    for r in row_order[:1]:
        for copy in loads(r):
            copy.start()

    def remote(index):
        side = SIDES[index]
        back = opposite(side)
        return pltpu.make_async_remote_copy(
            src_ref=at_region(rhs, own_edge(side[0], tile_rows), own_edge(side[1], tile_cols)),
            dst_ref=at_region(padded, outer_edge(back[0], tile_rows), outer_edge(back[1], tile_cols)),
            send_sem=send_sem.at[index],
            recv_sem=recv_sem.at[index],
            device_id=device(side),
            device_id_type=MESH,
        )

    greet(inside, device)
    for index, side in enumerate(SIDES):

        @pl.when(inside(side))
        def _():
            remote(index).start()

    centre_copy.start()
    for r in row_order[1:]:
        for copy in loads(r):
            copy.start()

    def mix(source, shift, r, c):
        parts = []
        for k in range(depth // points):
            code = cond[r, c, k]
            parts.append(source[r + code // SPAN + shift, c + lax.rem(code, SPAN) + shift])
        parts.append(source[r + REACH + shift, c + REACH + shift])
        mixed = jnp.dot(
            jnp.concatenate(parts, axis=1), weights[r, c], preferred_element_type=jnp.float32
        )
        white[r, c] = mixed.astype(white.dtype)

    inner_cols = list(range(REACH, tile_cols - REACH))
    outer_cols = [c for c in range(tile_cols) if c not in inner_cols]

    local_copy.wait()
    for r in range(REACH, tile_rows - REACH):
        for copy in loads(r):
            copy.wait()

    @pl.loop(REACH, tile_rows - REACH)
    def _(r):
        for c in inner_cols:
            mix(local, -REACH, r, c)

    centre_copy.wait()
    for r in range(tile_rows):
        if r < REACH or r >= tile_rows - REACH:
            for copy in loads(r):
                copy.wait()
    for index, side in enumerate(SIDES):

        @pl.when(inside(opposite(side)))
        def _():
            remote(index).wait_recv()

    @pl.loop(REACH, tile_rows - REACH)
    def _(r):
        for c in outer_cols:
            mix(padded, 0, r, c)

    @pl.loop(0, 2 * REACH)
    def _(step):
        r = jnp.where(step < REACH, step, tile_rows - 2 * REACH + step)
        for c in range(tile_cols):
            mix(padded, 0, r, c)

    for index, side in enumerate(SIDES):

        @pl.when(inside(side))
        def _():
            remote(index).wait_send()


def backward_kernel(white, diag, far, cond, own, halo, total):
    r = pl.program_id(0)
    tile_rows = pl.num_programs(0)
    tile_cols, count_rhs, points = white.shape[1:]
    conds = far.shape[2] // points
    across = (((1,), (1,)), ((), ()))

    @pl.when(r == 0)
    def _():
        @pl.loop(0, total.shape[0])
        def _(i):
            total[i] = jnp.zeros(total.shape[1:], jnp.float32)

    for c in range(tile_cols):
        value = white[0, c]
        spread = lax.dot_general(value, far[0, c], across, preferred_element_type=jnp.float32)
        kept = lax.dot_general(value, diag[0, c], across, preferred_element_type=jnp.float32)
        places = []
        for k in range(conds):
            code = cond[r, c, k]
            places.append((r + code // SPAN, c + lax.rem(code, SPAN)))
        places.append((r + REACH, c + REACH))
        held = [total[i, j] for i, j in places]
        for k, (i, j) in enumerate(places):
            term = kept if k == conds else spread[:, k * points : (k + 1) * points]
            total[i, j] = held[k] + term

    @pl.when(r == tile_rows - 1)
    def _():
        rows = own.shape[0]

        @pl.loop(0, rows + 2 * REACH)
        def _(i):
            for j in list(range(REACH)) + list(range(tile_cols + REACH, tile_cols + 2 * REACH)):
                halo[i, j] = total[i, j].astype(halo.dtype)

        @pl.loop(0, 2 * REACH)
        def _(step):
            i = jnp.where(step < REACH, step, rows + step)
            for j in range(REACH, tile_cols + REACH):
                halo[i, j] = total[i, j].astype(halo.dtype)

        @pl.loop(0, rows)
        def _(i):
            for j in range(tile_cols):
                own[i, j] = total[i + REACH, j + REACH]


def exchange_kernel(halo, *refs):
    landings, (send_sem, recv_sem) = refs[: len(SIDES)], refs[len(SIDES) :]
    tile_rows, tile_cols = halo.shape[0] - 2 * REACH, halo.shape[1] - 2 * REACH
    inside, device = neighbourhood()

    def remote(index):
        side = SIDES[index]
        return pltpu.make_async_remote_copy(
            src_ref=at_region(halo, outer_edge(side[0], tile_rows), outer_edge(side[1], tile_cols)),
            dst_ref=landings[index],
            send_sem=send_sem.at[index],
            recv_sem=recv_sem.at[index],
            device_id=device(side),
            device_id_type=MESH,
        )

    greet(inside, device)
    for index, side in enumerate(SIDES):

        @pl.when(inside(side))
        def _():
            remote(index).start()

    for index, side in enumerate(SIDES):

        @pl.when(inside(opposite(side)))
        def _():
            remote(index).wait_recv()

        @pl.when(inside(side))
        def _():
            remote(index).wait_send()


def finish_kernel(own, *refs):
    landings, out = refs[: len(SIDES)], refs[len(SIDES)]
    tile_rows, tile_cols = own.shape[:2]
    inside, _ = neighbourhood()

    @pl.loop(0, tile_rows)
    def _(i):
        out[i] = own[i]

    for index, side in enumerate(SIDES):
        back = opposite(side)
        row_start, row_count = own_edge(back[0], tile_rows)
        col_start, col_count = own_edge(back[1], tile_cols)

        @pl.when(inside(back))
        def _():
            @pl.loop(0, row_count)
            def _(i):
                for j in range(col_count):
                    out[row_start + i, col_start + j] += landings[index][i, j].astype(jnp.float32)


def shards(rhs_blocks, diag_factor, cond_factor, cond):
    tile_rows, tile_cols, count_rhs, points = rhs_blocks.shape
    conds = cond.shape[2]
    depth = conds * points
    far = cond_factor.reshape(tile_rows, tile_cols, depth, points)
    block = (count_rhs, points)
    padded = (tile_rows + 2 * REACH, tile_cols + 2 * REACH) + block
    anywhere = pl.BlockSpec(memory_space=pl.ANY)
    scalars = pl.BlockSpec(memory_space=pltpu.SMEM)
    whole = pl.BlockSpec(memory_space=pltpu.VMEM)
    sides = len(SIDES)
    white = pl.pallas_call(
        forward_kernel,
        out_shape=jax.ShapeDtypeStruct(rhs_blocks.shape, jnp.bfloat16),
        in_specs=[anywhere, anywhere, anywhere, scalars],
        out_specs=whole,
        scratch_shapes=[
            pltpu.VMEM(rhs_blocks.shape, rhs_blocks.dtype),
            pltpu.VMEM(padded, rhs_blocks.dtype),
            pltpu.VMEM((tile_rows, tile_cols, depth + points, points), far.dtype),
            pltpu.SemaphoreType.DMA((tile_rows, 2)),
            pltpu.SemaphoreType.DMA((2,)),
            pltpu.SemaphoreType.DMA((sides,)),
            pltpu.SemaphoreType.DMA((sides,)),
        ],
        compiler_params=pltpu.CompilerParams(
            collective_id=0, has_side_effects=True, vmem_limit_bytes=40 * 2**20
        ),
        name="forward",
    )(rhs_blocks, diag_factor, far, cond)

    own, halo = pl.pallas_call(
        backward_kernel,
        out_shape=(
            jax.ShapeDtypeStruct(rhs_blocks.shape, jnp.float32),
            jax.ShapeDtypeStruct(padded, jnp.bfloat16),
        ),
        grid=(tile_rows,),
        in_specs=[
            pl.BlockSpec((1, tile_cols) + block, lambda r: (r, 0, 0, 0)),
            pl.BlockSpec((1, tile_cols, points, points), lambda r: (r, 0, 0, 0)),
            pl.BlockSpec((1, tile_cols, depth, points), lambda r: (r, 0, 0, 0)),
            scalars,
        ],
        out_specs=(whole, whole),
        scratch_shapes=[pltpu.VMEM(padded, jnp.float32)],
        compiler_params=pltpu.CompilerParams(vmem_limit_bytes=40 * 2**20),
        name="backward",
    )(white, diag_factor, far, cond)

    landing = []
    for side in SIDES:
        part = (own_edge(side[0], tile_rows)[1], own_edge(side[1], tile_cols)[1])
        landing.append(jax.ShapeDtypeStruct(part + block, jnp.bfloat16))
    landed = pl.pallas_call(
        exchange_kernel,
        out_shape=tuple(landing),
        in_specs=[anywhere],
        out_specs=tuple(anywhere for _ in SIDES),
        scratch_shapes=[pltpu.SemaphoreType.DMA((sides,)), pltpu.SemaphoreType.DMA((sides,))],
        compiler_params=pltpu.CompilerParams(collective_id=1, has_side_effects=True),
        name="exchange",
    )(halo)

    return pl.pallas_call(
        finish_kernel,
        out_shape=jax.ShapeDtypeStruct(rhs_blocks.shape, jnp.float32),
        in_specs=[whole] * (1 + sides),
        out_specs=whole,
        compiler_params=pltpu.CompilerParams(vmem_limit_bytes=40 * 2**20),
        name="finish",
    )(own, *landed)


def solution(mesh):
    in_specs = (
        P("gx", "gy", None, None),
        P("gx", "gy", None, None),
        P("gx", "gy", None, None, None),
        P("gx", "gy", None),
    )
    out_specs = P("gx", "gy", None, None)
    return jax.shard_map(shards, mesh=mesh, in_specs=in_specs, out_specs=out_specs, check_vma=False)
```

time: 208 us -> 70.7 us (0.34)
  other arithmetic: 68.8 us -> 0 us
  Pallas kernels: 0 us -> 57.7 us
  matrix products: 45 us -> 0 us
  local copies, waits for them, and re-layouts: 41 us -> 12.2 us
  waiting for transfers between devices: 26.7 us -> 0 us
  starting transfers between devices: 23.5 us -> 0 us
    pallas_call x0 -> x4, Pallas kernels: none -> 57.7 us  [the longest x1 24.6 us: shards(): pl.pallas_call(forward_kernel, out_shape=jax.ShapeDtypeStruct(rhs_blocks....]
    dot_general x4 -> x0, matrix products: 45 us -> none  [the longest x1 22.1 us: shards(): jnp.einsum('xykrp,xykpq->xyrq', picked, cond_factor, preferred_element_ty...]
    reduce_sum x1 -> x0, other arithmetic: 37.4 us -> none  [shards(): contrib = jnp.sum(jnp.where(matched, spread, 0.0), axis=2)]
    ppermute x8 -> x0, waiting for transfers between devices: 26.7 us -> none  [the longest x4 22.7 us: from_behind(): lax.ppermute(value, axis, [(source, source + steps) for source in range(f...]
    ppermute x8 -> x0, starting transfers between devices: 23.5 us -> none  [the longest x4 11.6 us: from_behind(): lax.ppermute(value, axis, [(source, source + steps) for source in range(f...]
    scatter-add x27 -> x0, other arithmetic: 22.9 us -> none  [the longest x23 22.3 us: shards(): accumulated = accumulated.at[off_row:off_row + tile_rows, off_col:off_col...]
    eq x24 -> x0, local copies, waits for them, and re-layouts: 11.6 us -> none  [shards(): cond == code]
    concatenate x3 -> x0, other arithmetic: 7.05 us -> none  [extended(): jnp.concatenate([lax.ppermute(tail, axis, [(i, (i + 1) % count) for i in...]
  transfers between devices with their start and end apart: 8 -> 0, of which waited for: 5 -> 0; matrix products, arithmetic and copies ran while one was open for 13% -> 0% of each run, Pallas kernels for 0% -> 0%
where the time goes in v1:
time: 70.7 us; the launch traced here: 70 us
  Pallas kernels  57.7 us (82%)
  local copies, waits for them, and re-layouts  12.2 us (17%)
    pallas_call x1, Pallas kernels, shards(): pl.pallas_call(forward_kernel, out_shape=jax.ShapeDtypeStruct(rhs_blocks....  24.6 us
    pallas_call x1, Pallas kernels, shards(): pl.pallas_call(exchange_kernel, out_shape=tuple(landing), in_specs=[anywh...  20.3 us
    unnamed x25, local copies, waits for them, and re-layouts  12.2 us
    pallas_call x1, Pallas kernels, shards(): pl.pallas_call(backward_kernel, out_shape=(jax.ShapeDtypeStruct(rhs_block...  11 us
    pallas_call x1, Pallas kernels, shards(): pl.pallas_call(finish_kernel, out_shape=jax.ShapeDtypeStruct(rhs_blocks.s...  1.82 us

profile of v1, /device:TPU:9, one launch (start us, length us, event | category | flops | bytes accessed | tf_op | source)
XLA Modules:
  0.0 70.0 jit_solution(5925822785271595931)
XLA Ops:
  0.0 0.9 %copy.5.cond = s32[8,8,6]{2,1,0:T(8,128)S(1)} copy(s32[8,8,6]{1,0,2:T(8,128)} %param.7) | data formatting | bytes 3072 | tf_op args[3]
  0.9 0.0 copy-start
  0.9 1.6 %copy-done = bf16[8,8,128,128]{3,2,1,0:T(8,128)(2,1)S(1)} copy-done((bf16[8,8,128,128]{3,2,1,0:T(8,128)(2,1)S(1)}, bf16[8,8,128,128]{3,2,1,0:T(8,128)(2,1)}, u32[]{:S(2)}) %copy-start) | copy-done | bytes 2097176
  2.4 0.0 copy-start.3
  2.4 1.2 %copy-done.3 = bf16[8,8,64,128]{3,2,1,0:T(8,128)(2,1)S(1)} copy-done((bf16[8,8,64,128]{3,2,1,0:T(8,128)(2,1)S(1)}, bf16[8,8,64,128]{3,2,1,0:T(8,128)(2,1)}, u32[]{:S(2)}) %copy-start.3) | copy-done | bytes 1048600
  3.7 0.0 copy-start.1
  3.7 24.6 %forward.1.white = bf16[8,8,64,128]{3,2,1,0:T(8,128)(2,1)S(1)} custom-call(bf16[8,8,64,128]{3,2,1,0:T(8,128)(2,1)S(1)} %copy-done.3, bf16[8,8,128,128]{3,2,1,0:T(8,128)(2,1)S(1)} %copy-done, bf16[8,8,768,128]{3,2,1,0:T(8,128)(2,1)} %bitcast.1, s32[8,8,6]{2,1,0:T(8,128)S(1)} %copy.5.cond), custom_call_target="tpu_custom_call" | custom-call | tf_op jit(solution)/shard_map/forward/pallas_call | solution.py:273
  28.3 0.0 copy-done.1
  28.3 11.0 %backward.1 = (f32[8,8,64,128]{3,2,1,0:T(8,128)S(1)}, bf16[12,12,64,128]{3,2,1,0:T(8,128)(2,1)S(1)}) custom-call(bf16[8,8,64,128]{3,2,1,0:T(8,128)(2,1)S(1)} %forward.1.white, bf16[8,8,128,128]{3,2,1,0:T(8,128)(2,1)S(1)} %copy-done.1, bf16[8,8,768,128]{3,2,1,0:T(8,128)(2,1)} %bitcast.2, s32[8,8,6]{2,1,0:T(8,128)S(1)} %copy.5.cond), custom_call_target="tpu_custom_call" | custom-call | tf_op jit(solution)/shard_map/backward/pallas_call | solution.py:293
  39.3 0.0 copy-start.2
  39.3 1.4 %copy-done.2 = bf16[12,12,64,128]{3,2,1,0:T(8,128)(2,1)} copy-done((bf16[12,12,64,128]{3,2,1,0:T(8,128)(2,1)}, bf16[12,12,64,128]{3,2,1,0:T(8,128)(2,1)S(1)}, u32[]{:S(2)}) %copy-start.2) | copy-done | bytes 2359320
  40.7 20.3 %exchange.1 = (bf16[8,2,64,128]{3,2,1,0:T(8,128)(2,1)}, bf16[8,2,64,128]{3,2,1,0:T(8,128)(2,1)}, bf16[2,8,64,128]{3,2,1,0:T(8,128)(2,1)}, bf16[2,8,64,128]{3,2,1...) custom-call(bf16[12,12,64,128]{3,2,1,0:T(8,128)(2,1)} %copy-done.2), custom_call_target="tpu_custom_call" | custom-call | tf_op jit(solution)/shard_map/exchange/pallas_call | solution.py:316
  61.0 0.0 copy-start.4
  61.0 0.9 %copy-done.4 = bf16[8,2,64,128]{3,2,1,0:T(8,128)(2,1)S(1)} copy-done((bf16[8,2,64,128]{3,2,1,0:T(8,128)(2,1)S(1)}, bf16[8,2,64,128]{3,2,1,0:T(8,128)(2,1)}, u32[]{:S(2)}) %copy-start.4) | copy-done | bytes 262168
  62.0 0.0 copy-start.5
  62.0 0.9 %copy-done.5 = bf16[8,2,64,128]{3,2,1,0:T(8,128)(2,1)S(1)} copy-done((bf16[8,2,64,128]{3,2,1,0:T(8,128)(2,1)S(1)}, bf16[8,2,64,128]{3,2,1,0:T(8,128)(2,1)}, u32[]{:S(2)}) %copy-start.5) | copy-done | bytes 262168
  62.9 0.9 %copy-done.6 = bf16[2,8,64,128]{3,2,1,0:T(8,128)(2,1)S(1)} copy-done((bf16[2,8,64,128]{3,2,1,0:T(8,128)(2,1)S(1)}, bf16[2,8,64,128]{3,2,1,0:T(8,128)(2,1)}, u32[]{:S(2)}) %copy-start.6) | copy-done | bytes 262168
  63.9 0.0 copy-start.7
  63.9 0.9 %copy-done.7 = bf16[2,8,64,128]{3,2,1,0:T(8,128)(2,1)S(1)} copy-done((bf16[2,8,64,128]{3,2,1,0:T(8,128)(2,1)S(1)}, bf16[2,8,64,128]{3,2,1,0:T(8,128)(2,1)}, u32[]{:S(2)}) %copy-start.7) | copy-done | bytes 262168
  64.8 0.8 %copy-done.8 = bf16[2,2,64,128]{3,2,1,0:T(8,128)(2,1)S(1)} copy-done((bf16[2,2,64,128]{3,2,1,0:T(8,128)(2,1)S(1)}, bf16[2,2,64,128]{3,2,1,0:T(8,128)(2,1)}, u32[]{:S(2)}) %copy-start.8) | copy-done | bytes 65560
  65.7 0.8 %copy-done.9 = bf16[2,2,64,128]{3,2,1,0:T(8,128)(2,1)S(1)} copy-done((bf16[2,2,64,128]{3,2,1,0:T(8,128)(2,1)S(1)}, bf16[2,2,64,128]{3,2,1,0:T(8,128)(2,1)}, u32[]{:S(2)}) %copy-start.9) | copy-done | bytes 65560
  66.5 0.8 %copy-done.10 = bf16[2,2,64,128]{3,2,1,0:T(8,128)(2,1)S(1)} copy-done((bf16[2,2,64,128]{3,2,1,0:T(8,128)(2,1)S(1)}, bf16[2,2,64,128]{3,2,1,0:T(8,128)(2,1)}, u32[]{:S(2)}) %copy-start.10) | copy-done | bytes 65560
  67.4 0.8 %copy-done.11 = bf16[2,2,64,128]{3,2,1,0:T(8,128)(2,1)S(1)} copy-done((bf16[2,2,64,128]{3,2,1,0:T(8,128)(2,1)S(1)}, bf16[2,2,64,128]{3,2,1,0:T(8,128)(2,1)}, u32[]{:S(2)}) %copy-start.11) | copy-done | bytes 65560
  68.2 1.8 %finish.1 = f32[8,8,64,128]{3,2,1,0:T(8,128)} custom-call(f32[8,8,64,128]{3,2,1,0:T(8,128)S(1)} %get-tuple-element.15.own, bf16[8,2,64,128]{3,2,1,0:T(8,128)(2,1)S(1)} %copy-done.4, bf16[8,2,64,128]{3,2,1,0:T(8,128)(2,1)S(1)} %copy-done.5, bf16[2,8,64,128]{3,2,1,0:T(8,128)(2,1)S(1)} %copy-done.6, bf16[2,8,64,128]{3,2,1,0:T(8,128)(2,1)S(1)} %copy-done.7, ...), custom_call_target="tpu_custom_call" | custom-call | tf_op jit(solution)/shard_map/finish/pallas_call | solution.py:326
  (5 shorter events, 0.0 us)
Async XLA Ops:
  0.9 1.6 %copy-start = (bf16[8,8,128,128]{3,2,1,0:T(8,128)(2,1)S(1)}, bf16[8,8,128,128]{3,2,1,0:T(8,128)(2,1)}, u32[]{:S(2)}) copy-start(bf16[8,8,128,128]{3,2,1,0:T(8,128)(2,1)} %diag.3) | copy-start | bytes 6291460
  2.4 1.2 %copy-start.3 = (bf16[8,8,64,128]{3,2,1,0:T(8,128)(2,1)S(1)}, bf16[8,8,64,128]{3,2,1,0:T(8,128)(2,1)}, u32[]{:S(2)}) copy-start(bf16[8,8,64,128]{3,2,1,0:T(8,128)(2,1)} %rhs.1) | copy-start | bytes 3145732
  3.7 24.7 %copy-start.1 = (bf16[8,8,128,128]{3,2,1,0:T(8,128)(2,1)S(1)}, bf16[8,8,128,128]{3,2,1,0:T(8,128)(2,1)}, u32[]{:S(2)}) copy-start(bf16[8,8,128,128]{3,2,1,0:T(8,128)(2,1)} %diag.3) | copy-start | bytes 6291460
  39.3 1.4 %copy-start.2 = (bf16[12,12,64,128]{3,2,1,0:T(8,128)(2,1)}, bf16[12,12,64,128]{3,2,1,0:T(8,128)(2,1)S(1)}, u32[]{:S(2)}) copy-start(bf16[12,12,64,128]{3,2,1,0:T(8,128)(2,1)S(1)} %get-tuple-element.16.halo) | copy-start | bytes 7077892
  61.0 1.0 %copy-start.4 = (bf16[8,2,64,128]{3,2,1,0:T(8,128)(2,1)S(1)}, bf16[8,2,64,128]{3,2,1,0:T(8,128)(2,1)}, u32[]{:S(2)}) copy-start(bf16[8,2,64,128]{3,2,1,0:T(8,128)(2,1)} %get-tuple-element.17.refs_0_) | copy-start | bytes 786436
  62.0 0.9 %copy-start.5 = (bf16[8,2,64,128]{3,2,1,0:T(8,128)(2,1)S(1)}, bf16[8,2,64,128]{3,2,1,0:T(8,128)(2,1)}, u32[]{:S(2)}) copy-start(bf16[8,2,64,128]{3,2,1,0:T(8,128)(2,1)} %get-tuple-element.18.refs_1_) | copy-start | bytes 786436
  62.9 0.9 %copy-start.6 = (bf16[2,8,64,128]{3,2,1,0:T(8,128)(2,1)S(1)}, bf16[2,8,64,128]{3,2,1,0:T(8,128)(2,1)}, u32[]{:S(2)}) copy-start(bf16[2,8,64,128]{3,2,1,0:T(8,128)(2,1)} %get-tuple-element.19.refs_2_) | copy-start | bytes 786436
  63.9 0.9 %copy-start.7 = (bf16[2,8,64,128]{3,2,1,0:T(8,128)(2,1)S(1)}, bf16[2,8,64,128]{3,2,1,0:T(8,128)(2,1)}, u32[]{:S(2)}) copy-start(bf16[2,8,64,128]{3,2,1,0:T(8,128)(2,1)} %get-tuple-element.20.refs_3_) | copy-start | bytes 786436
  64.8 0.8 %copy-start.8 = (bf16[2,2,64,128]{3,2,1,0:T(8,128)(2,1)S(1)}, bf16[2,2,64,128]{3,2,1,0:T(8,128)(2,1)}, u32[]{:S(2)}) copy-start(bf16[2,2,64,128]{3,2,1,0:T(8,128)(2,1)} %get-tuple-element.21.refs_4_) | copy-start | bytes 196612
  65.7 0.8 %copy-start.9 = (bf16[2,2,64,128]{3,2,1,0:T(8,128)(2,1)S(1)}, bf16[2,2,64,128]{3,2,1,0:T(8,128)(2,1)}, u32[]{:S(2)}) copy-start(bf16[2,2,64,128]{3,2,1,0:T(8,128)(2,1)} %get-tuple-element.22.refs_5_) | copy-start | bytes 196612
  66.5 0.8 %copy-start.10 = (bf16[2,2,64,128]{3,2,1,0:T(8,128)(2,1)S(1)}, bf16[2,2,64,128]{3,2,1,0:T(8,128)(2,1)}, u32[]{:S(2)}) copy-start(bf16[2,2,64,128]{3,2,1,0:T(8,128)(2,1)} %get-tuple-element.23.refs_6_) | copy-start | bytes 196612
  67.4 0.8 %copy-start.11 = (bf16[2,2,64,128]{3,2,1,0:T(8,128)(2,1)S(1)}, bf16[2,2,64,128]{3,2,1,0:T(8,128)(2,1)}, u32[]{:S(2)}) copy-start(bf16[2,2,64,128]{3,2,1,0:T(8,128)(2,1)} %get-tuple-element.24.refs_7_) | copy-start | bytes 196612

commit v2 on v1

v2 whole, which is shorter than its diff:
```python
import functools

import jax
import jax.numpy as jnp
from jax import lax
from jax.experimental import pallas as pl
from jax.experimental.pallas import tpu as pltpu
from jax.sharding import PartitionSpec as P

MESH = pl.DeviceIdType.MESH
REACH = 2
SPAN = 2 * REACH + 1
ROW_SIDES = [(-1, 0), (1, 0)]
COL_SIDES = [(0, -1), (0, 1)]
SIDES = ROW_SIDES + COL_SIDES


def own_edge(step, size):
    return {-1: (0, REACH), 0: (0, size), 1: (size - REACH, REACH)}[step]


def outer_edge(step, size):
    return {-1: (0, REACH), 0: (REACH, size), 1: (REACH + size, REACH)}[step]


def at_region(ref, row_part, col_part):
    return ref.at[pl.ds(*row_part), pl.ds(*col_part)]


def neighbourhood():
    row, col = lax.axis_index("gx"), lax.axis_index("gy")
    rows, cols = lax.axis_size("gx"), lax.axis_size("gy")

    def inside(side):
        r, c = row + side[0], col + side[1]
        return (r >= 0) & (r < rows) & (c >= 0) & (c < cols)

    def device(side):
        return {"gx": row + side[0], "gy": col + side[1]}

    return inside, device


def greet(inside, device):
    barrier = pltpu.get_barrier_semaphore()
    count = jnp.int32(0)
    for side in SIDES:
        count = count + inside(side).astype(jnp.int32)

        @pl.when(inside(side))
        def _():
            pl.semaphore_signal(barrier, inc=1, device_id=device(side), device_id_type=MESH)

    pl.semaphore_wait(barrier, count)


def opposite(side):
    return (-side[0], -side[1])


def transfer(src, dst, send_sem, recv_sem, index, device, side):
    return pltpu.make_async_remote_copy(
        src_ref=src,
        dst_ref=dst,
        send_sem=send_sem.at[index],
        recv_sem=recv_sem.at[index],
        device_id=device(side),
        device_id_type=MESH,
    )


def start_if(inside, side, copies):
    @pl.when(inside(side))
    def _():
        for copy in copies():
            copy.start()


def wait_recv_if(inside, side, copies):
    @pl.when(inside(opposite(side)))
    def _():
        for copy in copies():
            copy.wait_recv()


def wait_send_if(inside, side, copies):
    @pl.when(inside(side))
    def _():
        for copy in copies():
            copy.wait_send()


def forward_kernel(rhs, diag, far, cond, white, local, rowed, padded, weights, load_sem, rhs_sem, send_sem, recv_sem):
    tile_rows, tile_cols, count_rhs, points = rhs.shape
    depth = far.shape[2]
    inside, device = neighbourhood()
    row_order = list(range(REACH, tile_rows - REACH))
    row_order += [r for r in range(tile_rows) if r not in row_order]
    sends = (send_sem, recv_sem)
    middle = (REACH, tile_rows - 2 * REACH)

    def loads(r):
        return [
            pltpu.make_async_copy(far.at[r], weights.at[r, :, pl.ds(0, depth)], load_sem.at[r, 0]),
            pltpu.make_async_copy(diag.at[r], weights.at[r, :, pl.ds(depth, points)], load_sem.at[r, 1]),
        ]

    local_copy = pltpu.make_async_copy(rhs, local, rhs_sem.at[0])
    centre_copy = pltpu.make_async_copy(rhs, rowed.at[pl.ds(REACH, tile_rows)], rhs_sem.at[1])
    padded_copy = pltpu.make_async_copy(
        rowed, padded.at[:, pl.ds(REACH, tile_cols)], rhs_sem.at[2]
    )

    def row_copies(side):
        return [
            transfer(
                rhs.at[pl.ds(*own_edge(side[0], tile_rows))],
                rowed.at[pl.ds(*outer_edge(-side[0], tile_rows))],
                *sends, 0 if side[0] < 0 else 1, device, side,
            )
        ]

    def col_copy(side, part, index):
        return transfer(
            at_region(rhs, part, own_edge(side[1], tile_cols)),
            at_region(padded, (part[0] + REACH, part[1]), outer_edge(-side[1], tile_cols)),
            *sends, index + (0 if side[1] < 0 else 1), device, side,
        )

    def col_ends(side):
        return [
            col_copy(side, own_edge(-1, tile_rows), 2),
            col_copy(side, own_edge(1, tile_rows), 4),
        ]

    def col_middle(side):
        return [col_copy(side, middle, 6)]

    def corner_copy(side, col_side):
        start, count = own_edge(side[0], tile_rows)
        cols = outer_edge(col_side[1], tile_cols)
        return transfer(
            at_region(padded, (start + REACH, count), cols),
            at_region(padded, outer_edge(-side[0], tile_rows), cols),
            *sends,
            8 + (0 if side[0] < 0 else 1) + (0 if col_side[1] < 0 else 2),
            device, side,
        )

    local_copy.start()
    for copy in loads(row_order[0]):
        copy.start()
    greet(inside, device)
    for side in COL_SIDES:
        start_if(inside, side, lambda: col_ends(side))
    for side in COL_SIDES:
        start_if(inside, side, lambda: col_middle(side))
    for side in ROW_SIDES:
        start_if(inside, side, lambda: row_copies(side))
    centre_copy.start()
    for r in row_order[1:]:
        for copy in loads(r):
            copy.start()

    def mix(source, row_shift, col_shift, r, c):
        parts = []
        for k in range(depth // points):
            code = cond[r, c, k]
            parts.append(source[r + code // SPAN + row_shift, c + lax.rem(code, SPAN) + col_shift])
        parts.append(source[r + REACH + row_shift, c + REACH + col_shift])
        mixed = jnp.dot(
            jnp.concatenate(parts, axis=1), weights[r, c], preferred_element_type=jnp.float32
        )
        white[r, c] = mixed.astype(white.dtype)

    inner_cols = list(range(REACH, tile_cols - REACH))
    outer_cols = [c for c in range(tile_cols) if c not in inner_cols]

    local_copy.wait()
    for r in range(REACH, tile_rows - REACH):
        for copy in loads(r):
            copy.wait()

    @pl.loop(REACH, tile_rows - REACH)
    def _(r):
        for c in inner_cols:
            mix(local, -REACH, -REACH, r, c)

    centre_copy.wait()
    for side in ROW_SIDES:
        wait_recv_if(inside, side, lambda: row_copies(side))
    padded_copy.start()

    for col_side in COL_SIDES:
        wait_recv_if(inside, opposite(col_side), lambda: col_ends(opposite(col_side)))
        for side in ROW_SIDES:

            @pl.when(inside(side) & inside(col_side))
            def _():
                corner_copy(side, col_side).start()

    for r in range(tile_rows):
        if r < REACH or r >= tile_rows - REACH:
            for copy in loads(r):
                copy.wait()

    @pl.loop(0, 2 * REACH)
    def _(step):
        r = jnp.where(step < REACH, step, tile_rows - 2 * REACH + step)
        for c in inner_cols:
            mix(rowed, 0, -REACH, r, c)

    padded_copy.wait()
    for side in COL_SIDES:
        wait_recv_if(inside, side, lambda: col_middle(side))
    for col_side in COL_SIDES:
        for side in ROW_SIDES:

            @pl.when(inside(opposite(side)) & inside(col_side))
            def _():
                corner_copy(side, col_side).wait_recv()

    @pl.loop(0, tile_rows)
    def _(r):
        for c in outer_cols:
            mix(padded, 0, 0, r, c)

    for side in COL_SIDES:
        wait_send_if(inside, side, lambda: col_ends(side) + col_middle(side))
    for side in ROW_SIDES:
        wait_send_if(inside, side, lambda: row_copies(side))
        for col_side in COL_SIDES:

            @pl.when(inside(side) & inside(col_side))
            def _():
                corner_copy(side, col_side).wait_send()


def backward_kernel(white, diag, far, cond, own, halo, total):
    r = pl.program_id(0)
    tile_cols, count_rhs, points = white.shape[1:]
    tile_rows = pl.num_programs(0) - 2 * REACH
    conds = far.shape[2] // points
    across = (((1,), (1,)), ((), ()))

    def clear(i):
        total[i] = jnp.zeros(total.shape[1:], jnp.float32)

    @pl.when(r == 0)
    def _():
        pl.loop(0, 2 * REACH)(clear)

    @pl.when(r < tile_rows)
    def _():
        clear(r + 2 * REACH)
        for c in range(tile_cols):
            value = white[0, c]
            spread = lax.dot_general(value, far[0, c], across, preferred_element_type=jnp.float32)
            kept = lax.dot_general(value, diag[0, c], across, preferred_element_type=jnp.float32)
            places = []
            for k in range(conds):
                code = cond[r, c, k]
                places.append((r + code // SPAN, c + lax.rem(code, SPAN)))
            places.append((r + REACH, c + REACH))
            held = [total[i, j] for i, j in places]
            for k, (i, j) in enumerate(places):
                term = kept if k == conds else spread[:, k * points : (k + 1) * points]
                total[i, j] = held[k] + term

    for j in range(tile_cols + 2 * REACH):
        halo[0, j] = total[r, j].astype(halo.dtype)
    @pl.when(r < tile_rows + REACH)
    def _():
        for j in range(tile_cols):
            own[0, j] = total[r, j + REACH]


def exchange_kernel(halo, landed_up, landed_down, landed_left, landed_right, edges, corners, edge_sem, send_sem, recv_sem):
    tile_rows, tile_cols = landed_left.shape[0], landed_up.shape[1]
    inside, device = neighbourhood()
    sends = (send_sem, recv_sem)
    middle = (REACH, tile_rows - 2 * REACH)

    def place(side):
        return 0 if side[0] + side[1] < 0 else 1

    def row_copies(side):
        return [
            transfer(
                at_region(halo, outer_edge(side[0], tile_rows), (REACH, tile_cols)),
                landed_down if side[0] < 0 else landed_up,
                *sends, place(side), device, side,
            )
        ]

    def corner_copies(side):
        return [
            transfer(
                at_region(halo, outer_edge(side[0], tile_rows), outer_edge(col_side[1], tile_cols)),
                corners.at[place(opposite(side)), place(col_side)],
                *sends, 2 + place(side) + 2 * place(col_side), device, side,
            )
            for col_side in COL_SIDES
        ]

    def col_landing(side):
        return landed_right if side[1] < 0 else landed_left

    def col_middle(side):
        return [
            transfer(
                at_region(halo, (middle[0] + REACH, middle[1]), outer_edge(side[1], tile_cols)),
                col_landing(side).at[pl.ds(*middle)],
                *sends, 6 + place(side), device, side,
            )
        ]

    def col_end(side, row_side):
        return transfer(
            edges.at[place(row_side), place(side)],
            col_landing(side).at[pl.ds(*own_edge(row_side[0], tile_rows))],
            *sends, 8 + place(side) + 2 * place(row_side), device, side,
        )

    def col_ends(side):
        return [col_end(side, row_side) for row_side in ROW_SIDES]

    def edge_copy(row_side, side):
        start, count = own_edge(row_side[0], tile_rows)
        return pltpu.make_async_copy(
            at_region(halo, (start + REACH, count), outer_edge(side[1], tile_cols)),
            edges.at[place(row_side), place(side)],
            edge_sem.at[place(row_side) + 2 * place(side)],
        )

    for row_side in ROW_SIDES:
        for side in COL_SIDES:
            edge_copy(row_side, side).start()
    greet(inside, device)
    for side in ROW_SIDES:
        start_if(inside, side, lambda: corner_copies(side))
    for side in COL_SIDES:
        start_if(inside, side, lambda: col_middle(side))
    for side in ROW_SIDES:
        start_if(inside, side, lambda: row_copies(side))
    for row_side in ROW_SIDES:
        row = place(row_side)
        wait_recv_if(inside, opposite(row_side), lambda: corner_copies(opposite(row_side)))
        for side in COL_SIDES:
            col = place(side)
            edge_copy(row_side, side).wait()

            @pl.when(inside(row_side))
            def _():
                for i in range(REACH):
                    for j in range(REACH):
                        term = corners[row, col, i, j].astype(jnp.float32)
                        value = edges[row, col, i, j].astype(jnp.float32) + term
                        edges[row, col, i, j] = value.astype(edges.dtype)

            @pl.when(inside(side))
            def _():
                col_end(side, row_side).start()

    for side in ROW_SIDES:
        wait_recv_if(inside, side, lambda: row_copies(side))
        wait_send_if(inside, side, lambda: row_copies(side) + corner_copies(side))
    for side in COL_SIDES:
        wait_recv_if(inside, side, lambda: col_middle(side) + col_ends(side))
        wait_send_if(inside, side, lambda: col_middle(side) + col_ends(side))


def finish_kernel(own, landed_up, landed_down, landed_left, landed_right, out):
    r = pl.program_id(0)
    tile_rows, tile_cols = pl.num_programs(0), own.shape[1]
    inside, _ = neighbourhood()
    out[...] = own[...]

    for side, landed in zip(COL_SIDES, (landed_left, landed_right)):
        start, count = own_edge(side[1], tile_cols)

        @pl.when(inside(side))
        def _():
            out[0, pl.ds(start, count)] += landed[r].astype(jnp.float32)

    for side, landed in zip(ROW_SIDES, (landed_up, landed_down)):
        start, count = own_edge(side[0], tile_rows)

        @pl.when(inside(side) & (r >= start) & (r < start + count))
        def _():
            out[0] += landed[r - start].astype(jnp.float32)


def shards(rhs_blocks, diag_factor, cond_factor, cond):
    tile_rows, tile_cols, count_rhs, points = rhs_blocks.shape
    conds = cond.shape[2]
    depth = conds * points
    far = cond_factor.reshape(tile_rows, tile_cols, depth, points)
    block = (count_rhs, points)
    padded = (tile_rows + 2 * REACH, tile_cols + 2 * REACH) + block
    anywhere = pl.BlockSpec(memory_space=pltpu.HBM)
    scalars = pl.BlockSpec(memory_space=pltpu.SMEM)
    whole = pl.BlockSpec(memory_space=pltpu.VMEM)
    transfers = 12
    white = pl.pallas_call(
        forward_kernel,
        out_shape=jax.ShapeDtypeStruct(rhs_blocks.shape, jnp.bfloat16),
        in_specs=[anywhere, anywhere, anywhere, scalars],
        out_specs=whole,
        scratch_shapes=[
            pltpu.VMEM(rhs_blocks.shape, rhs_blocks.dtype),
            pltpu.VMEM((tile_rows + 2 * REACH, tile_cols) + block, rhs_blocks.dtype),
            pltpu.VMEM(padded, rhs_blocks.dtype),
            pltpu.VMEM((tile_rows, tile_cols, depth + points, points), far.dtype),
            pltpu.SemaphoreType.DMA((tile_rows, 2)),
            pltpu.SemaphoreType.DMA((3,)),
            pltpu.SemaphoreType.DMA((transfers,)),
            pltpu.SemaphoreType.DMA((transfers,)),
        ],
        compiler_params=pltpu.CompilerParams(
            collective_id=0, has_side_effects=True, vmem_limit_bytes=63 * 2**20
        ),
        name="forward",
    )(rhs_blocks, diag_factor, far, cond)

    own, halo = pl.pallas_call(
        backward_kernel,
        out_shape=(
            jax.ShapeDtypeStruct(rhs_blocks.shape, jnp.float32),
            jax.ShapeDtypeStruct(padded, jnp.bfloat16),
        ),
        grid=(tile_rows + 2 * REACH,),
        in_specs=[
            pl.BlockSpec((1, tile_cols) + block, lambda r: (jnp.minimum(r, tile_rows - 1), 0, 0, 0)),
            pl.BlockSpec((1, tile_cols, points, points), lambda r: (jnp.minimum(r, tile_rows - 1), 0, 0, 0)),
            pl.BlockSpec((1, tile_cols, depth, points), lambda r: (jnp.minimum(r, tile_rows - 1), 0, 0, 0)),
            scalars,
        ],
        out_specs=(
            pl.BlockSpec((1, tile_cols) + block, lambda r: (jnp.clip(r - REACH, 0, tile_rows - 1), 0, 0, 0)),
            pl.BlockSpec((1, tile_cols + 2 * REACH) + block, lambda r: (r, 0, 0, 0)),
        ),
        scratch_shapes=[pltpu.VMEM(padded, jnp.float32)],
        compiler_params=pltpu.CompilerParams(vmem_limit_bytes=63 * 2**20),
        name="backward",
    )(white, diag_factor, far, cond)

    row_part = jax.ShapeDtypeStruct((REACH, tile_cols) + block, jnp.bfloat16)
    col_part = jax.ShapeDtypeStruct((tile_rows, REACH) + block, jnp.bfloat16)
    landed = pl.pallas_call(
        exchange_kernel,
        out_shape=(row_part, row_part, col_part, col_part),
        in_specs=[anywhere],
        out_specs=(whole,) * 4,
        scratch_shapes=[
            pltpu.VMEM((2, 2, REACH, REACH) + block, jnp.bfloat16),
            pltpu.VMEM((2, 2, REACH, REACH) + block, jnp.bfloat16),
            pltpu.SemaphoreType.DMA((4,)),
            pltpu.SemaphoreType.DMA((transfers,)),
            pltpu.SemaphoreType.DMA((transfers,)),
        ],
        compiler_params=pltpu.CompilerParams(
            collective_id=1, has_side_effects=True, vmem_limit_bytes=62 * 2**20
        ),
        name="exchange",
    )(halo)

    return pl.pallas_call(
        finish_kernel,
        out_shape=jax.ShapeDtypeStruct(rhs_blocks.shape, jnp.float32),
        grid=(tile_rows,),
        in_specs=[pl.BlockSpec((1, tile_cols) + block, lambda r: (r, 0, 0, 0))] + [whole] * 4,
        out_specs=pl.BlockSpec((1, tile_cols) + block, lambda r: (r, 0, 0, 0)),
        compiler_params=pltpu.CompilerParams(vmem_limit_bytes=62 * 2**20),
        name="finish",
    )(own, *landed)


def solution(mesh):
    in_specs = (
        P("gx", "gy", None, None),
        P("gx", "gy", None, None),
        P("gx", "gy", None, None, None),
        P("gx", "gy", None),
    )
    out_specs = P("gx", "gy", None, None)
    return jax.shard_map(shards, mesh=mesh, in_specs=in_specs, out_specs=out_specs, check_vma=False)
```

time: 70.7 us -> 59.7 us (0.84)
  local copies, waits for them, and re-layouts: 12.2 us -> 1.47 us
    unnamed x25 -> x1, local copies, waits for them, and re-layouts: 12.2 us -> 1.47 us
    pallas_call x1, Pallas kernels: 1.82 us -> 6.15 us  [shards(): pl.pallas_call(finish_kernel, out_shape=jax.ShapeDtypeStruct(rhs_blocks.s...]
    pallas_call x1, Pallas kernels: 20.3 us -> 16.3 us  [shards(): pl.pallas_call(exchange_kernel, out_shape=(row_part, row_part, col_part,...]
    pallas_call x1, Pallas kernels: 24.6 us -> 21.2 us  [shards(): pl.pallas_call(forward_kernel, out_shape=jax.ShapeDtypeStruct(rhs_blocks....]
    pallas_call x1, Pallas kernels: 11 us -> 14 us  [shards(): pl.pallas_call(backward_kernel, out_shape=(jax.ShapeDtypeStruct(rhs_block...]
where the time goes in v2:
time: 59.7 us; the launch traced here: 59.1 us
  Pallas kernels  57.6 us (96%)
  local copies, waits for them, and re-layouts  1.47 us (2%)
    pallas_call x1, Pallas kernels, shards(): pl.pallas_call(forward_kernel, out_shape=jax.ShapeDtypeStruct(rhs_blocks....  21.2 us
    pallas_call x1, Pallas kernels, shards(): pl.pallas_call(exchange_kernel, out_shape=(row_part, row_part, col_part,...  16.3 us
    pallas_call x1, Pallas kernels, shards(): pl.pallas_call(backward_kernel, out_shape=(jax.ShapeDtypeStruct(rhs_block...  14 us
    pallas_call x1, Pallas kernels, shards(): pl.pallas_call(finish_kernel, out_shape=jax.ShapeDtypeStruct(rhs_blocks.s...  6.15 us
    unnamed x1, local copies, waits for them, and re-layouts  1.47 us

profile of v2, /device:TPU:9, one launch (start us, length us, event | category | flops | bytes accessed | tf_op | source)
XLA Modules:
  0.0 59.1 jit_solution(16199489967950534780)
XLA Ops:
  0.0 1.5 %copy.5.cond = s32[8,8,6]{2,1,0:T(8,128)} copy(s32[8,8,6]{1,0,2:T(8,128)} %param.7) | data formatting | bytes 3072 | tf_op args[3]
  1.5 21.2 %forward.1.white = bf16[8,8,64,128]{3,2,1,0:T(8,128)(2,1)} custom-call(bf16[8,8,64,128]{3,2,1,0:T(8,128)(2,1)} %rhs.1, bf16[8,8,128,128]{3,2,1,0:T(8,128)(2,1)} %diag.3, bf16[8,8,768,128]{3,2,1,0:T(8,128)(2,1)} %bitcast.1, s32[8,8,6]{2,1,0:T(8,128)} %copy.5.cond), custom_call_target="tpu_custom_call" | custom-call | tf_op jit(solution)/shard_map/forward/pallas_call | solution.py:405
  22.7 14.0 %backward.1 = (f32[8,8,64,128]{3,2,1,0:T(8,128)}, bf16[12,12,64,128]{3,2,1,0:T(8,128)(2,1)}) custom-call(bf16[8,8,64,128]{3,2,1,0:T(8,128)(2,1)} %forward.1.white, bf16[8,8,128,128]{3,2,1,0:T(8,128)(2,1)} %diag.3, bf16[8,8,768,128]{3,2,1,0:T(8,128)(2,1)} %bitcast.2, s32[8,8,6]{2,1,0:T(8,128)} %copy.5.cond), custom_call_target="tpu_custom_call" | custom-call | tf_op jit(solution)/shard_map/backward/pallas_call | solution.py:426
  36.6 16.3 %exchange.1 = (bf16[2,8,64,128]{3,2,1,0:T(8,128)(2,1)}, bf16[2,8,64,128]{3,2,1,0:T(8,128)(2,1)}, bf16[8,2,64,128]{3,2,1,0:T(8,128)(2,1)}, bf16[8,2,64,128]{3,2,1,0:T(8,128)(2,1)}) custom-call(bf16[12,12,64,128]{3,2,1,0:T(8,128)(2,1)} %get-tuple-element.12.halo), custom_call_target="tpu_custom_call" | custom-call | tf_op jit(solution)/shard_map/exchange/pallas_call | solution.py:450
  52.9 6.2 %finish.1 = f32[8,8,64,128]{3,2,1,0:T(8,128)} custom-call(f32[8,8,64,128]{3,2,1,0:T(8,128)} %get-tuple-element.11.own, bf16[2,8,64,128]{3,2,1,0:T(8,128)(2,1)} %get-tuple-element.13.landed_up, bf16[2,8,64,128]{3,2,1,0:T(8,128)(2,1)} %get-tuple-element.14.landed_down, bf16[8,2,64,128]{3,2,1,0:T(8,128)(2,1)} %get-tuple-element.15.landed_left, ...), custom_call_target="tpu_custom_call" | custom-call | tf_op jit(solution)/shard_map/finish/pallas_call | solution.py:468

commit v3 on v2

--- a/solution.py
+++ b/solution.py
@@ -10,6 +10,7 @@
 MESH = pl.DeviceIdType.MESH
 REACH = 2
 SPAN = 2 * REACH + 1
+ACROSS = (((1,), (1,)), ((), ()))
 ROW_SIDES = [(-1, 0), (1, 0)]
 COL_SIDES = [(0, -1), (0, 1)]
 SIDES = ROW_SIDES + COL_SIDES
@@ -90,7 +91,9 @@
             copy.wait_send()
 
 
-def forward_kernel(rhs, diag, far, cond, white, local, rowed, padded, weights, load_sem, rhs_sem, send_sem, recv_sem):
+def forward_kernel(
+    rhs, diag, far, cond, white, spread_out, local, rowed, padded, weights, spread, spread_sem, load_sem, rhs_sem, send_sem, recv_sem
+):
     tile_rows, tile_cols, count_rhs, points = rhs.shape
     depth = far.shape[2]
     inside, device = neighbourhood()
@@ -165,13 +168,24 @@
     def mix(source, row_shift, col_shift, r, c):
         parts = []
         for k in range(depth // points):
-            code = cond[r, c, k]
+            code = cond[k, r, c]
             parts.append(source[r + code // SPAN + row_shift, c + lax.rem(code, SPAN) + col_shift])
         parts.append(source[r + REACH + row_shift, c + REACH + col_shift])
         mixed = jnp.dot(
             jnp.concatenate(parts, axis=1), weights[r, c], preferred_element_type=jnp.float32
         )
-        white[r, c] = mixed.astype(white.dtype)
+        return mixed.astype(white.dtype)
+
+    def spread_copy(r):
+        return pltpu.make_async_copy(spread.at[r], spread_out.at[r], spread_sem.at[r])
+
+    def inner_row(source, row_shift, r):
+        for index, c in enumerate(inner_cols):
+            value = mix(source, row_shift, -REACH, r, c)
+            spread[r, index] = lax.dot_general(
+                value, weights[r, c], ACROSS, preferred_element_type=jnp.float32
+            )
+        spread_copy(r).start()
 
     inner_cols = list(range(REACH, tile_cols - REACH))
     outer_cols = [c for c in range(tile_cols) if c not in inner_cols]
@@ -183,8 +197,7 @@
 
     @pl.loop(REACH, tile_rows - REACH)
     def _(r):
-        for c in inner_cols:
-            mix(local, -REACH, -REACH, r, c)
+        inner_row(local, -REACH, r)
 
     centre_copy.wait()
     for side in ROW_SIDES:
@@ -207,8 +220,7 @@
     @pl.loop(0, 2 * REACH)
     def _(step):
         r = jnp.where(step < REACH, step, tile_rows - 2 * REACH + step)
-        for c in inner_cols:
-            mix(rowed, 0, -REACH, r, c)
+        inner_row(rowed, 0, r)
 
     padded_copy.wait()
     for side in COL_SIDES:
@@ -222,8 +234,9 @@
 
     @pl.loop(0, tile_rows)
     def _(r):
-        for c in outer_cols:
-            mix(padded, 0, 0, r, c)
+        for index, c in enumerate(outer_cols):
+            white[r, index] = mix(padded, 0, 0, r, c)
+        spread_copy(r).wait()
 
     for side in COL_SIDES:
         wait_send_if(inside, side, lambda: col_ends(side) + col_middle(side))
@@ -236,47 +249,104 @@
                 corner_copy(side, col_side).wait_send()
 
 
-def backward_kernel(white, diag, far, cond, own, halo, total):
-    r = pl.program_id(0)
-    tile_cols, count_rhs, points = white.shape[1:]
-    tile_rows = pl.num_programs(0) - 2 * REACH
-    conds = far.shape[2] // points
-    across = (((1,), (1,)), ((), ()))
-
-    def clear(i):
+def backward_kernel(
+    white, diag, far, spread, cond, own, halo, weights, spreads, total, own_out, halo_out, load_sem, own_sem, halo_sem
+):
+    tile_rows, tile_cols, points = diag.shape[:3]
+    depth = far.shape[2]
+    conds = depth // points
+    inner_cols = list(range(REACH, tile_cols - REACH))
+    outer_cols = [c for c in range(tile_cols) if c not in inner_cols]
+
+    def loads(r):
+        copies = [pltpu.make_async_copy(spread.at[r], spreads.at[r], load_sem.at[r, 0])]
+        for index, side in enumerate(COL_SIDES):
+            cols = pl.ds(*own_edge(side[1], tile_cols))
+            slots = pl.ds(index * REACH, REACH)
+            copies += [
+                pltpu.make_async_copy(
+                    far.at[r, cols], weights.at[r, slots, pl.ds(0, depth)], load_sem.at[r, 1 + 2 * index]
+                ),
+                pltpu.make_async_copy(
+                    diag.at[r, cols], weights.at[r, slots, pl.ds(depth, points)], load_sem.at[r, 2 + 2 * index]
+                ),
+            ]
+        return copies
+
+    @pl.loop(0, tile_rows)
+    def _(r):
+        for copy in loads(r):
+            copy.start()
+
+    @pl.loop(0, tile_rows + 2 * REACH)
+    def _(i):
         total[i] = jnp.zeros(total.shape[1:], jnp.float32)
 
-    @pl.when(r == 0)
-    def _():
-        pl.loop(0, 2 * REACH)(clear)
-
-    @pl.when(r < tile_rows)
-    def _():
-        clear(r + 2 * REACH)
-        for c in range(tile_cols):
-            value = white[0, c]
-            spread = lax.dot_general(value, far[0, c], across, preferred_element_type=jnp.float32)
-            kept = lax.dot_general(value, diag[0, c], across, preferred_element_type=jnp.float32)
-            places = []
-            for k in range(conds):
-                code = cond[r, c, k]
-                places.append((r + code // SPAN, c + lax.rem(code, SPAN)))
-            places.append((r + REACH, c + REACH))
-            held = [total[i, j] for i, j in places]
-            for k, (i, j) in enumerate(places):
-                term = kept if k == conds else spread[:, k * points : (k + 1) * points]
-                total[i, j] = held[k] + term
-
-    for j in range(tile_cols + 2 * REACH):
-        halo[0, j] = total[r, j].astype(halo.dtype)
-    @pl.when(r < tile_rows + REACH)
-    def _():
+    def halo_copy(i):
+        return pltpu.make_async_copy(halo_out.at[i], halo.at[i], halo_sem.at[i])
+
+    def own_copy(i):
+        return pltpu.make_async_copy(own_out.at[i], own.at[i], own_sem.at[i])
+
+    def emit_halo(i):
+        for j in range(tile_cols + 2 * REACH):
+            halo_out[i, j] = total[i, j].astype(halo.dtype)
+        halo_copy(i).start()
+
+    def emit_own(i):
         for j in range(tile_cols):
-            own[0, j] = total[r, j + REACH]
-
-
-def exchange_kernel(halo, landed_up, landed_down, landed_left, landed_right, edges, corners, edge_sem, send_sem, recv_sem):
-    tile_rows, tile_cols = landed_left.shape[0], landed_up.shape[1]
+            own_out[i, j] = total[i + REACH, j + REACH]
+        own_copy(i).start()
+
+    def add(r, c, terms):
+        places = []
+        for k in range(conds):
+            code = cond[k, r, c]
+            places.append((r + code // SPAN, c + lax.rem(code, SPAN)))
+        places.append((r + REACH, c + REACH))
+        held = [total[i, j] for i, j in places]
+        for k, (i, j) in enumerate(places):
+            total[i, j] = held[k] + terms[:, k * points : (k + 1) * points]
+
+    @pl.loop(0, tile_rows)
+    def _(r):
+        for copy in loads(r):
+            copy.wait()
+        for index, c in enumerate(outer_cols):
+            terms = lax.dot_general(
+                white[r, index], weights[r, index], ACROSS, preferred_element_type=jnp.float32
+            )
+            add(r, c, terms)
+        for index, c in enumerate(inner_cols):
+            add(r, c, spreads[r, index])
+
+        emit_halo(r)
+
+        @pl.when(r >= REACH)
+        def _():
+            emit_own(r - REACH)
+
+    @pl.loop(tile_rows, tile_rows + 2 * REACH)
+    def _(i):
+        emit_halo(i)
+
+        @pl.when(i < tile_rows + REACH)
+        def _():
+            emit_own(i - REACH)
+
+    @pl.loop(0, tile_rows + 2 * REACH)
+    def _(i):
+        halo_copy(i).wait()
+
+    @pl.loop(0, tile_rows)
+    def _(i):
+        own_copy(i).wait()
+
+
+def exchange_kernel(
+    halo, own, out, landed_up, landed_down, landed_left, landed_right, edges, corners, own_sem, edge_sem, send_sem, recv_sem
+):
+    tile_rows, tile_cols = own.shape[:2]
     inside, device = neighbourhood()
     sends = (send_sem, recv_sem)
     middle = (REACH, tile_rows - 2 * REACH)
@@ -333,9 +403,11 @@
             edge_sem.at[place(row_side) + 2 * place(side)],
         )
 
+    own_copy = pltpu.make_async_copy(own, out, own_sem)
     for row_side in ROW_SIDES:
         for side in COL_SIDES:
             edge_copy(row_side, side).start()
+    own_copy.start()
     greet(inside, device)
     for side in ROW_SIDES:
         start_if(inside, side, lambda: corner_copies(side))
@@ -362,33 +434,29 @@
             def _():
                 col_end(side, row_side).start()
 
+    def take(landed, side):
+        row_start, row_count = own_edge(side[0], tile_rows)
+        col_start, col_count = own_edge(side[1], tile_cols)
+
+        @pl.when(inside(side))
+        def _():
+            @pl.loop(0, row_count)
+            def _(i):
+                for j in range(col_count):
+                    out[row_start + i, col_start + j] += landed[i, j].astype(jnp.float32)
+
+    own_copy.wait()
+    for side, landed in zip(ROW_SIDES, (landed_up, landed_down)):
+        wait_recv_if(inside, opposite(side), lambda: row_copies(opposite(side)))
+        take(landed, side)
+    for side, landed in zip(COL_SIDES, (landed_left, landed_right)):
+        back = opposite(side)
+        wait_recv_if(inside, back, lambda: col_middle(back) + col_ends(back))
+        take(landed, side)
     for side in ROW_SIDES:
-        wait_recv_if(inside, side, lambda: row_copies(side))
         wait_send_if(inside, side, lambda: row_copies(side) + corner_copies(side))
     for side in COL_SIDES:
-        wait_recv_if(inside, side, lambda: col_middle(side) + col_ends(side))
         wait_send_if(inside, side, lambda: col_middle(side) + col_ends(side))
-
-
-def finish_kernel(own, landed_up, landed_down, landed_left, landed_right, out):
-    r = pl.program_id(0)
-    tile_rows, tile_cols = pl.num_programs(0), own.shape[1]
-    inside, _ = neighbourhood()
-    out[...] = own[...]
-
-    for side, landed in zip(COL_SIDES, (landed_left, landed_right)):
-        start, count = own_edge(side[1], tile_cols)
-
-        @pl.when(inside(side))
-        def _():
-            out[0, pl.ds(start, count)] += landed[r].astype(jnp.float32)
-
-    for side, landed in zip(ROW_SIDES, (landed_up, landed_down)):
-        start, count = own_edge(side[0], tile_rows)
-
-        @pl.when(inside(side) & (r >= start) & (r < start + count))
-        def _():
-            out[0] += landed[r - start].astype(jnp.float32)
 
 
 def shards(rhs_blocks, diag_factor, cond_factor, cond):
@@ -396,22 +464,31 @@
     conds = cond.shape[2]
     depth = conds * points
     far = cond_factor.reshape(tile_rows, tile_cols, depth, points)
+    codes = jnp.transpose(cond, (2, 0, 1))
     block = (count_rhs, points)
     padded = (tile_rows + 2 * REACH, tile_cols + 2 * REACH) + block
+    outer = 2 * REACH
+    inner = tile_cols - outer
+    spread_shape = (tile_rows, inner, count_rhs, depth + points)
     anywhere = pl.BlockSpec(memory_space=pltpu.HBM)
     scalars = pl.BlockSpec(memory_space=pltpu.SMEM)
     whole = pl.BlockSpec(memory_space=pltpu.VMEM)
     transfers = 12
-    white = pl.pallas_call(
+    white, spread = pl.pallas_call(
         forward_kernel,
-        out_shape=jax.ShapeDtypeStruct(rhs_blocks.shape, jnp.bfloat16),
+        out_shape=(
+            jax.ShapeDtypeStruct((tile_rows, outer) + block, jnp.bfloat16),
+            jax.ShapeDtypeStruct(spread_shape, jnp.float32),
+        ),
         in_specs=[anywhere, anywhere, anywhere, scalars],
-        out_specs=whole,
+        out_specs=(whole, anywhere),
         scratch_shapes=[
             pltpu.VMEM(rhs_blocks.shape, rhs_blocks.dtype),
             pltpu.VMEM((tile_rows + 2 * REACH, tile_cols) + block, rhs_blocks.dtype),
             pltpu.VMEM(padded, rhs_blocks.dtype),
             pltpu.VMEM((tile_rows, tile_cols, depth + points, points), far.dtype),
+            pltpu.VMEM(spread_shape, jnp.float32),
+            pltpu.SemaphoreType.DMA((tile_rows,)),
             pltpu.SemaphoreType.DMA((tile_rows, 2)),
             pltpu.SemaphoreType.DMA((3,)),
             pltpu.SemaphoreType.DMA((transfers,)),
@@ -421,7 +498,7 @@
             collective_id=0, has_side_effects=True, vmem_limit_bytes=63 * 2**20
         ),
         name="forward",
-    )(rhs_blocks, diag_factor, far, cond)
+    )(rhs_blocks, diag_factor, far, codes)
 
     own, halo = pl.pallas_call(
         backward_kernel,
@@ -429,51 +506,46 @@
             jax.ShapeDtypeStruct(rhs_blocks.shape, jnp.float32),
             jax.ShapeDtypeStruct(padded, jnp.bfloat16),
         ),
-        grid=(tile_rows + 2 * REACH,),
-        in_specs=[
-            pl.BlockSpec((1, tile_cols) + block, lambda r: (jnp.minimum(r, tile_rows - 1), 0, 0, 0)),
-            pl.BlockSpec((1, tile_cols, points, points), lambda r: (jnp.minimum(r, tile_rows - 1), 0, 0, 0)),
-            pl.BlockSpec((1, tile_cols, depth, points), lambda r: (jnp.minimum(r, tile_rows - 1), 0, 0, 0)),
-            scalars,
+        in_specs=[whole, anywhere, anywhere, anywhere, scalars],
+        out_specs=(anywhere, anywhere),
+        scratch_shapes=[
+            pltpu.VMEM((tile_rows, outer, depth + points, points), far.dtype),
+            pltpu.VMEM(spread_shape, jnp.float32),
+            pltpu.VMEM(padded, jnp.float32),
+            pltpu.VMEM(rhs_blocks.shape, jnp.float32),
+            pltpu.VMEM(padded, jnp.bfloat16),
+            pltpu.SemaphoreType.DMA((tile_rows, 5)),
+            pltpu.SemaphoreType.DMA((tile_rows,)),
+            pltpu.SemaphoreType.DMA((tile_rows + 2 * REACH,)),
         ],
-        out_specs=(
-            pl.BlockSpec((1, tile_cols) + block, lambda r: (jnp.clip(r - REACH, 0, tile_rows - 1), 0, 0, 0)),
-            pl.BlockSpec((1, tile_cols + 2 * REACH) + block, lambda r: (r, 0, 0, 0)),
-        ),
-        scratch_shapes=[pltpu.VMEM(padded, jnp.float32)],
         compiler_params=pltpu.CompilerParams(vmem_limit_bytes=63 * 2**20),
         name="backward",
-    )(white, diag_factor, far, cond)
-
-    row_part = jax.ShapeDtypeStruct((REACH, tile_cols) + block, jnp.bfloat16)
-    col_part = jax.ShapeDtypeStruct((tile_rows, REACH) + block, jnp.bfloat16)
-    landed = pl.pallas_call(
+    )(white, diag_factor, far, spread, codes)
+
+    row_part = pltpu.VMEM((REACH, tile_cols) + block, jnp.bfloat16)
+    col_part = pltpu.VMEM((tile_rows, REACH) + block, jnp.bfloat16)
+    return pl.pallas_call(
         exchange_kernel,
-        out_shape=(row_part, row_part, col_part, col_part),
-        in_specs=[anywhere],
-        out_specs=(whole,) * 4,
+        out_shape=jax.ShapeDtypeStruct(rhs_blocks.shape, jnp.float32),
+        in_specs=[anywhere, anywhere],
+        out_specs=whole,
         scratch_shapes=[
+            row_part,
+            row_part,
+            col_part,
+            col_part,
             pltpu.VMEM((2, 2, REACH, REACH) + block, jnp.bfloat16),
             pltpu.VMEM((2, 2, REACH, REACH) + block, jnp.bfloat16),
+            pltpu.SemaphoreType.DMA,
             pltpu.SemaphoreType.DMA((4,)),
             pltpu.SemaphoreType.DMA((transfers,)),
             pltpu.SemaphoreType.DMA((transfers,)),
         ],
         compiler_params=pltpu.CompilerParams(
-            collective_id=1, has_side_effects=True, vmem_limit_bytes=62 * 2**20
+            collective_id=1, has_side_effects=True, vmem_limit_bytes=61 * 2**20
         ),
         name="exchange",
-    )(halo)
-
-    return pl.pallas_call(
-        finish_kernel,
-        out_shape=jax.ShapeDtypeStruct(rhs_blocks.shape, jnp.float32),
-        grid=(tile_rows,),
-        in_specs=[pl.BlockSpec((1, tile_cols) + block, lambda r: (r, 0, 0, 0))] + [whole] * 4,
-        out_specs=pl.BlockSpec((1, tile_cols) + block, lambda r: (r, 0, 0, 0)),
-        compiler_params=pltpu.CompilerParams(vmem_limit_bytes=62 * 2**20),
-        name="finish",
-    )(own, *landed)
+    )(halo, own)
 
 
 def solution(mesh):

time: 59.7 us -> 51.6 us (0.86)
  Pallas kernels: 57.6 us -> 48.1 us
  local copies, waits for them, and re-layouts: 1.47 us -> 3.16 us
    pallas_call x3 -> x2, Pallas kernels: 43.6 us -> 38.5 us  [the longest x1 21.7 us: shards(): pl.pallas_call(forward_kernel, out_shape=(jax.ShapeDtypeStruct((tile_rows...]
    pallas_call x1, Pallas kernels: 14 us -> 9.6 us  [shards(): pl.pallas_call(backward_kernel, out_shape=(jax.ShapeDtypeStruct(rhs_block...]
    unnamed x1, local copies, waits for them, and re-layouts: 1.47 us -> 3.16 us
where the time goes in v3:
time: 51.6 us; the launch traced here: 51.2 us
  Pallas kernels  48.1 us (93%)
  local copies, waits for them, and re-layouts  3.16 us (6%)
    pallas_call x1, Pallas kernels, shards(): pl.pallas_call(forward_kernel, out_shape=(jax.ShapeDtypeStruct((tile_rows...  21.7 us
    pallas_call x1, Pallas kernels, shards(): pl.pallas_call(exchange_kernel, out_shape=jax.ShapeDtypeStruct(rhs_blocks...  16.7 us
    pallas_call x1, Pallas kernels, shards(): pl.pallas_call(backward_kernel, out_shape=(jax.ShapeDtypeStruct(rhs_block...  9.6 us
    unnamed x1, local copies, waits for them, and re-layouts  3.16 us

profile of v3, /device:TPU:9, one launch (start us, length us, event | category | flops | bytes accessed | tf_op | source)
XLA Modules:
  0.0 51.2 jit_solution(7469978547205689904)
XLA Ops:
  0.0 21.7 %forward.1 = (bf16[8,4,64,128]{3,2,1,0:T(8,128)(2,1)}, f32[8,4,64,896]{3,2,1,0:T(8,128)}) custom-call(bf16[8,8,64,128]{3,2,1,0:T(8,128)(2,1)} %rhs.1, bf16[8,8,128,128]{3,2,1,0:T(8,128)(2,1)} %diag.3, bf16[8,8,768,128]{3,2,1,0:T(8,128)(2,1)} %bitcast.2, s32[6,8,8]{2,1,0:T(8,128)} %bitcast.4), custom_call_target="tpu_custom_call" | custom-call | tf_op jit(solution)/shard_map/forward/pallas_call | solution.py:477
  21.7 9.6 %backward.1 = (f32[8,8,64,128]{3,2,1,0:T(8,128)}, bf16[12,12,64,128]{3,2,1,0:T(8,128)(2,1)}) custom-call(bf16[8,4,64,128]{3,2,1,0:T(8,128)(2,1)} %get-tuple-element.9.white, bf16[8,8,128,128]{3,2,1,0:T(8,128)(2,1)} %diag.3, bf16[8,8,768,128]{3,2,1,0:T(8,128)(2,1)} %bitcast.3, f32[8,4,64,896]{3,2,1,0:T(8,128)} %get-tuple-element.10.spread, s32[6,8,8]{2,1,0:T(8,128)} %bitcast.5), custom_call_target="tpu_custom_call" | custom-call | tf_op jit(solution)/shard_map/backward/pallas_call | solution.py:503
  31.4 16.7 %exchange.1 = f32[8,8,64,128]{3,2,1,0:T(8,128)} custom-call(bf16[12,12,64,128]{3,2,1,0:T(8,128)(2,1)} %get-tuple-element.11.halo, f32[8,8,64,128]{3,2,1,0:T(8,128)} %get-tuple-element.12.own), custom_call_target="tpu_custom_call" | custom-call | tf_op jit(solution)/shard_map/exchange/pallas_call | solution.py:527
  48.1 3.2 %copy.6 = f32[8,8,64,128]{3,2,1,0:T(8,128)} copy(f32[8,8,64,128]{3,2,1,0:T(8,128)} %exchange.1) | data formatting | bytes 4194304

commit v4 on v3

--- a/solution.py
+++ b/solution.py
@@ -92,7 +92,7 @@
 
 
 def forward_kernel(
-    rhs, diag, far, cond, white, spread_out, local, rowed, padded, weights, spread, spread_sem, load_sem, rhs_sem, send_sem, recv_sem
+    rhs, diag, far, cond, white, spread_out, local, rowed, wide, padded, weights, spread, spread_sem, load_sem, rhs_sem, send_sem, recv_sem
 ):
     tile_rows, tile_cols, count_rhs, points = rhs.shape
     depth = far.shape[2]
@@ -113,6 +113,15 @@
     padded_copy = pltpu.make_async_copy(
         rowed, padded.at[:, pl.ds(REACH, tile_cols)], rhs_sem.at[2]
     )
+    wide_copy = pltpu.make_async_copy(rhs, wide.at[:, pl.ds(REACH, tile_cols)], rhs_sem.at[3])
+
+    def side_copy(side):
+        cols = pl.ds(*outer_edge(side[1], tile_cols))
+        return pltpu.make_async_copy(
+            wide.at[:, cols],
+            padded.at[pl.ds(REACH, tile_rows), cols],
+            rhs_sem.at[4 + (0 if side[1] < 0 else 1)],
+        )
 
     def row_copies(side):
         return [
@@ -126,7 +135,7 @@
     def col_copy(side, part, index):
         return transfer(
             at_region(rhs, part, own_edge(side[1], tile_cols)),
-            at_region(padded, (part[0] + REACH, part[1]), outer_edge(-side[1], tile_cols)),
+            at_region(wide, part, outer_edge(-side[1], tile_cols)),
             *sends, index + (0 if side[1] < 0 else 1), device, side,
         )
 
@@ -143,7 +152,7 @@
         start, count = own_edge(side[0], tile_rows)
         cols = outer_edge(col_side[1], tile_cols)
         return transfer(
-            at_region(padded, (start + REACH, count), cols),
+            at_region(wide, (start, count), cols),
             at_region(padded, outer_edge(-side[0], tile_rows), cols),
             *sends,
             8 + (0 if side[0] < 0 else 1) + (0 if col_side[1] < 0 else 2),
@@ -161,6 +170,7 @@
     for side in ROW_SIDES:
         start_if(inside, side, lambda: row_copies(side))
     centre_copy.start()
+    wide_copy.start()
     for r in row_order[1:]:
         for copy in loads(r):
             copy.start()
@@ -222,9 +232,24 @@
         r = jnp.where(step < REACH, step, tile_rows - 2 * REACH + step)
         inner_row(rowed, 0, r)
 
+    def outer_row(source, row_shift, r):
+        for index, c in enumerate(outer_cols):
+            white[r, index] = mix(source, row_shift, 0, r, c)
+        spread_copy(r).wait()
+
+    wide_copy.wait()
+    for side in COL_SIDES:
+        wait_recv_if(inside, side, lambda: col_middle(side))
+    for side in COL_SIDES:
+        side_copy(side).start()
+
+    @pl.loop(REACH, tile_rows - REACH)
+    def _(r):
+        outer_row(wide, -REACH, r)
+
     padded_copy.wait()
     for side in COL_SIDES:
-        wait_recv_if(inside, side, lambda: col_middle(side))
+        side_copy(side).wait()
     for col_side in COL_SIDES:
         for side in ROW_SIDES:
 
@@ -232,11 +257,9 @@
             def _():
                 corner_copy(side, col_side).wait_recv()
 
-    @pl.loop(0, tile_rows)
-    def _(r):
-        for index, c in enumerate(outer_cols):
-            white[r, index] = mix(padded, 0, 0, r, c)
-        spread_copy(r).wait()
+    @pl.loop(0, 2 * REACH)
+    def _(step):
+        outer_row(padded, 0, jnp.where(step < REACH, step, tile_rows - 2 * REACH + step))
 
     for side in COL_SIDES:
         wait_send_if(inside, side, lambda: col_ends(side) + col_middle(side))
@@ -343,10 +366,8 @@
         own_copy(i).wait()
 
 
-def exchange_kernel(
-    halo, own, out, landed_up, landed_down, landed_left, landed_right, edges, corners, own_sem, edge_sem, send_sem, recv_sem
-):
-    tile_rows, tile_cols = own.shape[:2]
+def exchange_kernel(halo, landed_up, landed_down, landed_left, landed_right, edges, corners, edge_sem, send_sem, recv_sem):
+    tile_rows, tile_cols = landed_left.shape[0], landed_up.shape[1]
     inside, device = neighbourhood()
     sends = (send_sem, recv_sem)
     middle = (REACH, tile_rows - 2 * REACH)
@@ -403,11 +424,9 @@
             edge_sem.at[place(row_side) + 2 * place(side)],
         )
 
-    own_copy = pltpu.make_async_copy(own, out, own_sem)
     for row_side in ROW_SIDES:
         for side in COL_SIDES:
             edge_copy(row_side, side).start()
-    own_copy.start()
     greet(inside, device)
     for side in ROW_SIDES:
         start_if(inside, side, lambda: corner_copies(side))
@@ -434,29 +453,57 @@
             def _():
                 col_end(side, row_side).start()
 
-    def take(landed, side):
-        row_start, row_count = own_edge(side[0], tile_rows)
-        col_start, col_count = own_edge(side[1], tile_cols)
-
-        @pl.when(inside(side))
-        def _():
-            @pl.loop(0, row_count)
-            def _(i):
-                for j in range(col_count):
-                    out[row_start + i, col_start + j] += landed[i, j].astype(jnp.float32)
-
-    own_copy.wait()
-    for side, landed in zip(ROW_SIDES, (landed_up, landed_down)):
-        wait_recv_if(inside, opposite(side), lambda: row_copies(opposite(side)))
-        take(landed, side)
-    for side, landed in zip(COL_SIDES, (landed_left, landed_right)):
-        back = opposite(side)
-        wait_recv_if(inside, back, lambda: col_middle(back) + col_ends(back))
-        take(landed, side)
     for side in ROW_SIDES:
+        wait_recv_if(inside, side, lambda: row_copies(side))
         wait_send_if(inside, side, lambda: row_copies(side) + corner_copies(side))
     for side in COL_SIDES:
+        wait_recv_if(inside, side, lambda: col_middle(side) + col_ends(side))
         wait_send_if(inside, side, lambda: col_middle(side) + col_ends(side))
+
+
+def finish_kernel(own, *refs):
+    landed, out, held, parts = refs[:4], refs[4], refs[5], refs[6:10]
+    part_sem, load_sem, store_sem = refs[10:]
+    landed_up, landed_down, landed_left, landed_right = parts
+    tile_rows, tile_cols = own.shape[:2]
+    inside, _ = neighbourhood()
+
+    def load(i):
+        return pltpu.make_async_copy(own.at[i], held.at[i], load_sem.at[i])
+
+    def store(i):
+        return pltpu.make_async_copy(held.at[i], out.at[i], store_sem.at[i])
+
+    def fetch(index):
+        return pltpu.make_async_copy(landed[index], parts[index], part_sem.at[index])
+
+    load(0).start()
+    for index in range(4):
+        fetch(index).start()
+    for i in range(1, tile_rows):
+        load(i).start()
+    for index in range(4):
+        fetch(index).wait()
+    for i in range(tile_rows):
+        load(i).wait()
+        for side, part in zip(COL_SIDES, (landed_left, landed_right)):
+            start, count = own_edge(side[1], tile_cols)
+
+            @pl.when(inside(side))
+            def _():
+                held[i, pl.ds(start, count)] += part[i].astype(jnp.float32)
+
+        for side, part in zip(ROW_SIDES, (landed_up, landed_down)):
+            start, count = own_edge(side[0], tile_rows)
+            if start <= i < start + count:
+
+                @pl.when(inside(side))
+                def _():
+                    held[i] += part[i - start].astype(jnp.float32)
+
+        store(i).start()
+    for i in range(tile_rows):
+        store(i).wait()
 
 
 def shards(rhs_blocks, diag_factor, cond_factor, cond):
@@ -485,12 +532,13 @@
         scratch_shapes=[
             pltpu.VMEM(rhs_blocks.shape, rhs_blocks.dtype),
             pltpu.VMEM((tile_rows + 2 * REACH, tile_cols) + block, rhs_blocks.dtype),
+            pltpu.VMEM((tile_rows, tile_cols + 2 * REACH) + block, rhs_blocks.dtype),
             pltpu.VMEM(padded, rhs_blocks.dtype),
             pltpu.VMEM((tile_rows, tile_cols, depth + points, points), far.dtype),
             pltpu.VMEM(spread_shape, jnp.float32),
             pltpu.SemaphoreType.DMA((tile_rows,)),
             pltpu.SemaphoreType.DMA((tile_rows, 2)),
-            pltpu.SemaphoreType.DMA((3,)),
+            pltpu.SemaphoreType.DMA((6,)),
             pltpu.SemaphoreType.DMA((transfers,)),
             pltpu.SemaphoreType.DMA((transfers,)),
         ],
@@ -522,30 +570,44 @@
         name="backward",
     )(white, diag_factor, far, spread, codes)
 
-    row_part = pltpu.VMEM((REACH, tile_cols) + block, jnp.bfloat16)
-    col_part = pltpu.VMEM((tile_rows, REACH) + block, jnp.bfloat16)
-    return pl.pallas_call(
+    row_part = jax.ShapeDtypeStruct((REACH, tile_cols) + block, jnp.bfloat16)
+    col_part = jax.ShapeDtypeStruct((tile_rows, REACH) + block, jnp.bfloat16)
+    landed = pl.pallas_call(
         exchange_kernel,
-        out_shape=jax.ShapeDtypeStruct(rhs_blocks.shape, jnp.float32),
-        in_specs=[anywhere, anywhere],
-        out_specs=whole,
+        out_shape=(row_part, row_part, col_part, col_part),
+        in_specs=[anywhere],
+        out_specs=(anywhere,) * 4,
         scratch_shapes=[
-            row_part,
-            row_part,
-            col_part,
-            col_part,
             pltpu.VMEM((2, 2, REACH, REACH) + block, jnp.bfloat16),
             pltpu.VMEM((2, 2, REACH, REACH) + block, jnp.bfloat16),
-            pltpu.SemaphoreType.DMA,
             pltpu.SemaphoreType.DMA((4,)),
             pltpu.SemaphoreType.DMA((transfers,)),
             pltpu.SemaphoreType.DMA((transfers,)),
         ],
         compiler_params=pltpu.CompilerParams(
-            collective_id=1, has_side_effects=True, vmem_limit_bytes=61 * 2**20
+            collective_id=1, has_side_effects=True, vmem_limit_bytes=63 * 2**20
         ),
         name="exchange",
-    )(halo, own)
+    )(halo)
+
+    return pl.pallas_call(
+        finish_kernel,
+        out_shape=jax.ShapeDtypeStruct(rhs_blocks.shape, jnp.float32),
+        in_specs=[anywhere] * 5,
+        out_specs=anywhere,
+        scratch_shapes=[
+            pltpu.VMEM(rhs_blocks.shape, jnp.float32),
+            pltpu.VMEM(row_part.shape, row_part.dtype),
+            pltpu.VMEM(row_part.shape, row_part.dtype),
+            pltpu.VMEM(col_part.shape, col_part.dtype),
+            pltpu.VMEM(col_part.shape, col_part.dtype),
+            pltpu.SemaphoreType.DMA((4,)),
+            pltpu.SemaphoreType.DMA((tile_rows,)),
+            pltpu.SemaphoreType.DMA((tile_rows,)),
+        ],
+        compiler_params=pltpu.CompilerParams(vmem_limit_bytes=63 * 2**20),
+        name="finish",
+    )(own, *landed)
 
 
 def solution(mesh):

time: 51.6 us -> 50.5 us (0.979)
  local copies, waits for them, and re-layouts: 3.16 us -> 0 us
  Pallas kernels: 48.1 us -> 50.2 us
    unnamed x1 -> x0, local copies, waits for them, and re-layouts: 3.16 us -> none
    pallas_call x1 -> x2, Pallas kernels: 16.7 us -> 18.7 us  [the longest x1 15.4 us: shards(): pl.pallas_call(exchange_kernel, out_shape=(row_part, row_part, col_part,...]
where the time goes in v4:
time: 50.5 us; the launch traced here: 50.2 us
  Pallas kernels  50.2 us (99%)
    pallas_call x1, Pallas kernels, shards(): pl.pallas_call(forward_kernel, out_shape=(jax.ShapeDtypeStruct((tile_rows...  21.8 us
    pallas_call x1, Pallas kernels, shards(): pl.pallas_call(exchange_kernel, out_shape=(row_part, row_part, col_part,...  15.4 us
    pallas_call x1, Pallas kernels, shards(): pl.pallas_call(backward_kernel, out_shape=(jax.ShapeDtypeStruct(rhs_block...  9.71 us
    pallas_call x1, Pallas kernels, shards(): pl.pallas_call(finish_kernel, out_shape=jax.ShapeDtypeStruct(rhs_blocks.s...  3.26 us

profile of v4, /device:TPU:9, one launch (start us, length us, event | category | flops | bytes accessed | tf_op | source)
XLA Modules:
  0.0 50.2 jit_solution(10974208410562763811)
XLA Ops:
  0.0 21.8 %forward.1 = (bf16[8,4,64,128]{3,2,1,0:T(8,128)(2,1)}, f32[8,4,64,896]{3,2,1,0:T(8,128)}) custom-call(bf16[8,8,64,128]{3,2,1,0:T(8,128)(2,1)} %rhs.1, bf16[8,8,128,128]{3,2,1,0:T(8,128)(2,1)} %diag.3, bf16[8,8,768,128]{3,2,1,0:T(8,128)(2,1)} %bitcast.2, s32[6,8,8]{2,1,0:T(8,128)} %bitcast.4), custom_call_target="tpu_custom_call" | custom-call | tf_op jit(solution)/shard_map/forward/pallas_call | solution.py:524
  21.8 9.7 %backward.1 = (f32[8,8,64,128]{3,2,1,0:T(8,128)}, bf16[12,12,64,128]{3,2,1,0:T(8,128)(2,1)}) custom-call(bf16[8,4,64,128]{3,2,1,0:T(8,128)(2,1)} %get-tuple-element.13.white, bf16[8,8,128,128]{3,2,1,0:T(8,128)(2,1)} %diag.3, bf16[8,8,768,128]{3,2,1,0:T(8,128)(2,1)} %bitcast.3, f32[8,4,64,896]{3,2,1,0:T(8,128)} %get-tuple-element.14.spread, s32[6,8,8]{2,1,0:T(8,128)} %bitcast.5), custom_call_target="tpu_custom_call" | custom-call | tf_op jit(solution)/shard_map/backward/pallas_call | solution.py:551
  31.6 15.4 %exchange.1 = (bf16[2,8,64,128]{3,2,1,0:T(8,128)(2,1)}, bf16[2,8,64,128]{3,2,1,0:T(8,128)(2,1)}, bf16[8,2,64,128]{3,2,1,0:T(8,128)(2,1)}, bf16[8,2,64,128]{3,2,1,0:T(8,128)(2,1)}) custom-call(bf16[12,12,64,128]{3,2,1,0:T(8,128)(2,1)} %get-tuple-element.16.halo), custom_call_target="tpu_custom_call" | custom-call | tf_op jit(solution)/shard_map/exchange/pallas_call | solution.py:575
  47.0 3.3 %finish.1 = f32[8,8,64,128]{3,2,1,0:T(8,128)} custom-call(f32[8,8,64,128]{3,2,1,0:T(8,128)} %get-tuple-element.15.own, bf16[2,8,64,128]{3,2,1,0:T(8,128)(2,1)} %get-tuple-element.17.refs_0_, bf16[2,8,64,128]{3,2,1,0:T(8,128)(2,1)} %get-tuple-element.18.refs_1_, bf16[8,2,64,128]{3,2,1,0:T(8,128)(2,1)} %get-tuple-element.19.refs_2_, ...), custom_call_target="tpu_custom_call" | custom-call | tf_op jit(solution)/shard_map/finish/pallas_call | solution.py:593

commit v5 on v4

--- a/solution.py
+++ b/solution.py
@@ -14,6 +14,11 @@
 ROW_SIDES = [(-1, 0), (1, 0)]
 COL_SIDES = [(0, -1), (0, 1)]
 SIDES = ROW_SIDES + COL_SIDES
+
+
+def offsets(code):
+    off_row = (code * 13) >> 6
+    return off_row, code - off_row * SPAN
 
 
 def own_edge(step, size):
@@ -178,8 +183,8 @@
     def mix(source, row_shift, col_shift, r, c):
         parts = []
         for k in range(depth // points):
-            code = cond[k, r, c]
-            parts.append(source[r + code // SPAN + row_shift, c + lax.rem(code, SPAN) + col_shift])
+            off_row, off_col = offsets(cond[k, r, c])
+            parts.append(source[r + off_row + row_shift, c + off_col + col_shift])
         parts.append(source[r + REACH + row_shift, c + REACH + col_shift])
         mixed = jnp.dot(
             jnp.concatenate(parts, axis=1), weights[r, c], preferred_element_type=jnp.float32
@@ -205,7 +210,7 @@
         for copy in loads(r):
             copy.wait()
 
-    @pl.loop(REACH, tile_rows - REACH)
+    @pl.loop(REACH, tile_rows - REACH, unroll=2)
     def _(r):
         inner_row(local, -REACH, r)
 
@@ -227,7 +232,7 @@
             for copy in loads(r):
                 copy.wait()
 
-    @pl.loop(0, 2 * REACH)
+    @pl.loop(0, 2 * REACH, unroll=2)
     def _(step):
         r = jnp.where(step < REACH, step, tile_rows - 2 * REACH + step)
         inner_row(rowed, 0, r)
@@ -243,7 +248,7 @@
     for side in COL_SIDES:
         side_copy(side).start()
 
-    @pl.loop(REACH, tile_rows - REACH)
+    @pl.loop(REACH, tile_rows - REACH, unroll=2)
     def _(r):
         outer_row(wide, -REACH, r)
 
@@ -257,7 +262,7 @@
             def _():
                 corner_copy(side, col_side).wait_recv()
 
-    @pl.loop(0, 2 * REACH)
+    @pl.loop(0, 2 * REACH, unroll=2)
     def _(step):
         outer_row(padded, 0, jnp.where(step < REACH, step, tile_rows - 2 * REACH + step))
 
@@ -324,8 +329,8 @@
     def add(r, c, terms):
         places = []
         for k in range(conds):
-            code = cond[k, r, c]
-            places.append((r + code // SPAN, c + lax.rem(code, SPAN)))
+            off_row, off_col = offsets(cond[k, r, c])
+            places.append((r + off_row, c + off_col))
         places.append((r + REACH, c + REACH))
         held = [total[i, j] for i, j in places]
         for k, (i, j) in enumerate(places):

time: 50.5 us -> 49.8 us (0.986)
  Pallas kernels: 50.2 us -> 49.4 us
    pallas_call x1, Pallas kernels: 21.8 us -> 21.2 us  [shards(): pl.pallas_call(forward_kernel, out_shape=(jax.ShapeDtypeStruct((tile_rows...]
where the time goes in v5:
time: 49.8 us; the launch traced here: 49.5 us
  Pallas kernels  49.4 us (99%)
    pallas_call x1, Pallas kernels, shards(): pl.pallas_call(forward_kernel, out_shape=(jax.ShapeDtypeStruct((tile_rows...  21.2 us
    pallas_call x1, Pallas kernels, shards(): pl.pallas_call(exchange_kernel, out_shape=(row_part, row_part, col_part,...  15.4 us
    pallas_call x1, Pallas kernels, shards(): pl.pallas_call(backward_kernel, out_shape=(jax.ShapeDtypeStruct(rhs_block...  9.51 us
    pallas_call x1, Pallas kernels, shards(): pl.pallas_call(finish_kernel, out_shape=jax.ShapeDtypeStruct(rhs_blocks.s...  3.26 us

profile of v5, /device:TPU:9, one launch (start us, length us, event | category | flops | bytes accessed | tf_op | source)
XLA Modules:
  0.0 49.5 jit_solution(9051500629540486159)
XLA Ops:
  0.0 21.2 %forward.1 = (bf16[8,4,64,128]{3,2,1,0:T(8,128)(2,1)}, f32[8,4,64,896]{3,2,1,0:T(8,128)}) custom-call(bf16[8,8,64,128]{3,2,1,0:T(8,128)(2,1)} %rhs.1, bf16[8,8,128,128]{3,2,1,0:T(8,128)(2,1)} %diag.3, bf16[8,8,768,128]{3,2,1,0:T(8,128)(2,1)} %bitcast.2, s32[6,8,8]{2,1,0:T(8,128)} %bitcast.4), custom_call_target="tpu_custom_call" | custom-call | tf_op jit(solution)/shard_map/forward/pallas_call | solution.py:529
  21.3 9.5 %backward.1 = (f32[8,8,64,128]{3,2,1,0:T(8,128)}, bf16[12,12,64,128]{3,2,1,0:T(8,128)(2,1)}) custom-call(bf16[8,4,64,128]{3,2,1,0:T(8,128)(2,1)} %get-tuple-element.13.white, bf16[8,8,128,128]{3,2,1,0:T(8,128)(2,1)} %diag.3, bf16[8,8,768,128]{3,2,1,0:T(8,128)(2,1)} %bitcast.3, f32[8,4,64,896]{3,2,1,0:T(8,128)} %get-tuple-element.14.spread, s32[6,8,8]{2,1,0:T(8,128)} %bitcast.5), custom_call_target="tpu_custom_call" | custom-call | tf_op jit(solution)/shard_map/backward/pallas_call | solution.py:556
  30.8 15.4 %exchange.1 = (bf16[2,8,64,128]{3,2,1,0:T(8,128)(2,1)}, bf16[2,8,64,128]{3,2,1,0:T(8,128)(2,1)}, bf16[8,2,64,128]{3,2,1,0:T(8,128)(2,1)}, bf16[8,2,64,128]{3,2,1,0:T(8,128)(2,1)}) custom-call(bf16[12,12,64,128]{3,2,1,0:T(8,128)(2,1)} %get-tuple-element.16.halo), custom_call_target="tpu_custom_call" | custom-call | tf_op jit(solution)/shard_map/exchange/pallas_call | solution.py:580
  46.2 3.3 %finish.1 = f32[8,8,64,128]{3,2,1,0:T(8,128)} custom-call(f32[8,8,64,128]{3,2,1,0:T(8,128)} %get-tuple-element.15.own, bf16[2,8,64,128]{3,2,1,0:T(8,128)(2,1)} %get-tuple-element.17.refs_0_, bf16[2,8,64,128]{3,2,1,0:T(8,128)(2,1)} %get-tuple-element.18.refs_1_, bf16[8,2,64,128]{3,2,1,0:T(8,128)(2,1)} %get-tuple-element.19.refs_2_, ...), custom_call_target="tpu_custom_call" | custom-call | tf_op jit(solution)/shard_map/finish/pallas_call | solution.py:598
